TPU v7x, 32 devices: a whole 2x2x4 slice. The times are simulated.
32 devices in a mesh: dp: 8 (over z, y), band: 4 (over x, core).
Axes of the slice: x: 2, y: 2, z: 4, core: 2. Of those that a mesh axis runs over, the one named last changes fastest.
Arguments:
- cell_states: bfloat16 [16, 32, 128, 768], P('dp', 'band'), may hold values from -6 to 6
- head_grads: bfloat16 [16, 32, 128, 384], P('dp', 'band'), may hold values from -6 to 6
- group_ids: int32 [16, 128, 32], P('dp', 'band'), may hold values from 0 to 7, never falling along the last dimension, each value on 1 to 8 neighbouring positions
- proj_weights: bfloat16 [768, 1152], replicated, may hold values from -0.8694895 to 0.8694895
Outputs:
- input_grad: bfloat16 [16, 32, 128, 768], P('dp', 'band')
- weight_grad: float32 [768, 1152], P('band', 'dp')
Inputs may be any that keep to these rules, and one draw needn't show every extreme that they name: `group_ids`: group numbers never fall down the rows of a column; a cell sees the header row 0 and the cells of its own group.
All inputs are finite; a program needn't handle non-finite values.
Results may differ from a plain program's by a relative error of at most 0.008.
Values may be sent and summed in bfloat16 or wider, within the bound.
A program may use at most 128 MiB of HBM per device.

v0:
```python
import jax
import jax.numpy as jnp
from jax import lax
from jax.sharding import PartitionSpec as P

HD = 64


SCALE = 0.125
EPSILON = 1e-06


def normalize(states):
    widened = states.astype(jnp.float32)
    meansq = jnp.mean(widened * widened, axis=-1, keepdims=True)
    inverse = lax.rsqrt(meansq + EPSILON)
    scaled = widened * inverse
    return (scaled, inverse, scaled.astype(jnp.bfloat16))


def project(normed, weights):
    width = weights.shape[1] // 3
    flat = normed.reshape(-1, normed.shape[-1])
    mixed = jnp.dot(flat, weights, preferred_element_type=jnp.float32).astype(jnp.bfloat16)
    mixed = mixed.reshape(normed.shape[:-1] + (3 * width,))
    return (mixed[..., :width], mixed[..., width : 2 * width], mixed[..., 2 * width :])


def attend_back(query_rows, key_rows, value_rows, grad_rows, groups):
    shape = query_rows.shape
    split = shape[:-1] + (shape[-1] // HD, HD)
    query_five = query_rows.reshape(split)
    key_five = key_rows.reshape(split)
    value_five = value_rows.reshape(split)
    grad_five = grad_rows.reshape(split)
    scores = (
        jnp.einsum("bichd,bjchd->bchij", query_five, key_five, preferred_element_type=jnp.float32)
        * SCALE
    )
    header = lax.broadcasted_iota(jnp.int32, (shape[1], shape[1]), 1) == 0
    visible = (groups[:, :, :, None] == groups[:, :, None, :]) | header
    scores = jnp.where(visible[:, :, None], scores, -1e30)
    peak = jnp.max(scores, axis=-1, keepdims=True)
    expsc = jnp.exp(scores - peak)
    probs = expsc / jnp.sum(expsc, axis=-1, keepdims=True)
    probs_low = probs.astype(jnp.bfloat16)
    value_grad = jnp.einsum(
        "bchij,bichd->bjchd", probs_low, grad_five, preferred_element_type=jnp.float32
    ).astype(jnp.bfloat16)
    prob_grad = jnp.einsum(
        "bichd,bjchd->bchij", grad_five, value_five, preferred_element_type=jnp.float32
    )
    score_grad = probs * (prob_grad - jnp.sum(probs * prob_grad, axis=-1, keepdims=True))
    score_low = (score_grad * SCALE).astype(jnp.bfloat16)
    query_grad = jnp.einsum(
        "bchij,bjchd->bichd", score_low, key_five, preferred_element_type=jnp.float32
    ).astype(jnp.bfloat16)
    key_grad = jnp.einsum(
        "bchij,bichd->bjchd", score_low, query_five, preferred_element_type=jnp.float32
    ).astype(jnp.bfloat16)
    return (query_grad.reshape(shape), key_grad.reshape(shape), value_grad.reshape(shape))


def finish(scaled, inverse, normed, all_grads, weights):
    flat_norm = normed.reshape(-1, normed.shape[-1])
    flat_grad = all_grads.reshape(-1, all_grads.shape[-1])
    partial_w = lax.dot_general(
        flat_norm, flat_grad, (((0,), (0,)), ((), ())), preferred_element_type=jnp.float32
    )
    normed_grad = lax.dot_general(
        flat_grad, weights, (((1,), (1,)), ((), ())), preferred_element_type=jnp.float32
    )
    normed_grad = normed_grad.reshape(scaled.shape)
    coupling = jnp.mean(normed_grad * scaled, axis=-1, keepdims=True)
    state_grad = (inverse * (normed_grad - scaled * coupling)).astype(jnp.bfloat16)
    return (partial_w, state_grad)


def body(cell_states, head_grads, group_ids, proj_weights):
    scaled, inverse, normed = normalize(cell_states)
    query_rows, key_rows, value_rows = project(normed, proj_weights)
    query_cols, key_cols, value_cols, grad_cols = (
        lax.all_to_all(query_rows, "band", split_axis=2, concat_axis=1, tiled=True),
        lax.all_to_all(key_rows, "band", split_axis=2, concat_axis=1, tiled=True),
        lax.all_to_all(value_rows, "band", split_axis=2, concat_axis=1, tiled=True),
        lax.all_to_all(head_grads, "band", split_axis=2, concat_axis=1, tiled=True),
    )
    query_grad, key_grad, value_grad = attend_back(
        query_cols, key_cols, value_cols, grad_cols, group_ids
    )
    query_home, key_home, value_home = (
        lax.all_to_all(query_grad, "band", split_axis=1, concat_axis=2, tiled=True),
        lax.all_to_all(key_grad, "band", split_axis=1, concat_axis=2, tiled=True),
        lax.all_to_all(value_grad, "band", split_axis=1, concat_axis=2, tiled=True),
    )
    all_grads = jnp.concatenate((query_home, key_home, value_home), axis=-1)
    partial_w, input_grad = finish(scaled, inverse, normed, all_grads, proj_weights)
    shared = lax.psum_scatter(partial_w, "dp", scatter_dimension=1, tiled=True)
    weight_grad = lax.psum_scatter(shared, "band", scatter_dimension=0, tiled=True)
    return (input_grad, weight_grad)


def solution(mesh):
    return jax.shard_map(
        body,
        mesh=mesh,
        in_specs=(
            P("dp", "band", None, None),
            P("dp", "band", None, None),
            P("dp", "band", None),
            P(),
        ),
        out_specs=(P("dp", "band", None, None), P("band", "dp")),
        check_vma=False,
    )
```

profile of v0, /device:TPU:0, one launch (start us, length us, event | category | flops | bytes accessed | tf_op | source)
XLA Modules:
  0.0 372.7 jit_solution(2079444416898549724)
XLA Ops:
  7.2 0.0 copy-start
  7.2 0.0 copy-start.1
  7.2 2.7 fusion.9
  9.9 0.2 copy-done.1
  10.1 0.6 fusion.4
  10.8 4.5 %convolution_convert_fusion = bf16[2048,1152]{1,0:T(8,128)(2,1)S(1)} fusion(bf16[2048,768]{1,0:T(8,128)(2,1)S(1)} %bitcast.96, bf16[768,1152]{1,0:T(8,128)(2,1)S(1)} %copy-done), kind=kOutput, calls=%fused_computation.7 | convolution fusion | flops 3626237952 | bytes 9633792 | tf_op jit(solution)/shard_map/dot_general | solution.py:24
  15.2 2.3 fusion.43
  17.5 2.1 copy.93
  19.6 4.2 %all-to-all-start = ((bf16[2,8,128,384]{3,1,0,2:T(8,128)(2,1)}), bf16[2,8,128,384]{3,1,0,2:T(8,128)(2,1)S(1)}, u32[]{:S(2)}, u32[]{:S(2)}) async-start(bf16[2,8,128,384]{3,1,0,2:T(8,128)(2,1)} %copy.93), calls=%async_computation | async-start | bytes 3145728 | tf_op jit(solution)/shard_map/all_to_all | solution.py:84
  23.8 3.5 copy.94
  27.3 16.6 %all-to-all-done = bf16[2,8,128,384]{3,1,0,2:T(8,128)(2,1)S(1)} async-done(((bf16[2,8,128,384]{3,1,0,2:T(8,128)(2,1)}), bf16[2,8,128,384]{3,1,0,2:T(8,128)(2,1)S(1)}, u32[]{:S(2)}, u32[]{:S(2)}) %all-to-all-start) | async-done | bytes 1572896 | tf_op jit(solution)/shard_map/all_to_all | solution.py:84
  43.9 4.3 %all-to-all-start.1 = ((bf16[2,8,128,384]{3,1,0,2:T(8,128)(2,1)}), bf16[2,8,128,384]{3,1,0,2:T(8,128)(2,1)}, u32[]{:S(2)}, u32[]{:S(2)}) async-start(bf16[2,8,128,384]{3,1,0,2:T(8,128)(2,1)} %copy.94), calls=%async_computation.1 | async-start | bytes 3145728 | tf_op jit(solution)/shard_map/all_to_all | solution.py:83
  48.2 3.5 copy.95
  51.7 16.7 %all-to-all-done.1 = bf16[2,8,128,384]{3,1,0,2:T(8,128)(2,1)} async-done(((bf16[2,8,128,384]{3,1,0,2:T(8,128)(2,1)}), bf16[2,8,128,384]{3,1,0,2:T(8,128)(2,1)}, u32[]{:S(2)}, u32[]{:S(2)}) %all-to-all-start.1) | async-done | bytes 1572896 | tf_op jit(solution)/shard_map/all_to_all | solution.py:83
  68.4 4.3 %all-to-all-start.2 = ((bf16[2,8,128,384]{3,1,0,2:T(8,128)(2,1)}), bf16[2,8,128,384]{3,1,0,2:T(8,128)(2,1)}, u32[]{:S(2)}, u32[]{:S(2)}) async-start(bf16[2,8,128,384]{3,1,0,2:T(8,128)(2,1)} %copy.95), calls=%async_computation.2 | async-start | bytes 3145728 | tf_op jit(solution)/shard_map/all_to_all | solution.py:85
  72.7 3.5 copy.54
  76.2 16.7 %all-to-all-done.2 = bf16[2,8,128,384]{3,1,0,2:T(8,128)(2,1)} async-done(((bf16[2,8,128,384]{3,1,0,2:T(8,128)(2,1)}), bf16[2,8,128,384]{3,1,0,2:T(8,128)(2,1)}, u32[]{:S(2)}, u32[]{:S(2)}) %all-to-all-start.2) | async-done | bytes 1572896 | tf_op jit(solution)/shard_map/all_to_all | solution.py:85
  92.9 4.6 %all-to-all-start.3 = ((bf16[2,8,128,384]{3,1,0,2:T(8,128)(2,1)}), bf16[2,8,128,384]{3,1,0,2:T(8,128)(2,1)}, u32[]{:S(2)}, u32[]{:S(2)}) async-start(bf16[2,8,128,384]{3,1,0,2:T(8,128)(2,1)} %copy.54), calls=%async_computation.3 | async-start | bytes 3145728 | tf_op jit(solution)/shard_map/all_to_all | solution.py:86
  97.5 1.1 compare_or_fusion
  98.6 1.5 copy.45
  100.1 5.9 %reshape.72 = bf16[2,32,32,6,64]{4,3,2,1,0:T(8,128)(2,1)} reshape(bf16[2,4,8,32,384]{4,3,2,1,0:T(8,128)(2,1)} %copy.45) | data formatting | bytes 3145728 | tf_op jit(solution)/shard_map/reshape | solution.py:33
  106.0 1.7 copy.48
  107.8 3.7 %reshape.73 = bf16[2,32,32,6,64]{4,3,2,1,0:T(8,128)(2,1)} reshape(bf16[2,4,8,32,384]{4,3,2,1,0:T(8,128)(2,1)S(1)} %copy.48) | data formatting | bytes 3145728 | tf_op jit(solution)/shard_map/reshape | solution.py:32
  111.5 1.7 copy.53
  113.3 3.7 reshape.74
  117.0 0.6 all-to-all-done.3
  117.6 1.7 copy.111
  119.4 3.8 %reshape.75 = bf16[2,32,32,6,64]{4,3,2,1,0:T(8,128)(2,1)} reshape(bf16[2,4,8,32,384]{4,3,2,1,0:T(8,128)(2,1)S(1)} %bitcast.94) | data formatting | bytes 3145728 | tf_op jit(solution)/shard_map/reshape | solution.py:35
  123.1 7.5 %fusion.26 = f32[2,32,6,32,32]{3,4,2,1,0:T(8,128)S(1)} fusion(bf16[2,32,32,6,64]{4,3,2,1,0:T(8,128)(2,1)} %reshape.72, bf16[2,32,32,6,64]{4,3,2,1,0:T(8,128)(2,1)} %reshape.73), kind=kOutput, calls=%fused_computation.37 | convolution fusion | flops 50331648 | bytes 4718592 | tf_op jit(solution)/shard_map/bichd,bjchd->bchij/dot_general | solution.py:37
  130.7 4.7 %fusion.44 = (f32[2,32,6,32]{3,2,1,0:T(8,128)S(1)}, f32[2,32,6,32,32]{3,4,2,1,0:T(8,128)}) fusion(f32[2,32,6,32,32]{3,4,2,1,0:T(8,128)S(1)} %fusion.26, pred[2,32,32,32]{2,3,1,0:T(8,128)(4,1)S(1)} %copy-done.8), kind=kOutput, calls=%fused_computation.60 | output fusion | flops 2359327 | bytes 3260416 | tf_op jit(solution)/shard_map/sub | solution.py:44
  135.4 1.0 copy-done.4
  136.4 6.3 %fusion.14 = f32[2,32,6,32,32]{4,3,2,1,0:T(8,128)} fusion(bf16[2,32,32,6,64]{4,3,2,1,0:T(8,128)(2,1)S(1)} %copy-done.4, bf16[2,32,32,6,64]{4,3,2,1,0:T(8,128)(2,1)S(1)} %copy-done.3), kind=kOutput, calls=%fused_computation.23 | convolution fusion | flops 50331648 | bytes 4718592 | tf_op jit(solution)/shard_map/bichd,bjchd->bchij/dot_general | solution.py:50
  142.7 14.3 %convert_bitcast_fusion.2 = bf16[2,32,32,6,64]{4,1,3,2,0:T(8,128)(2,1)} fusion(f32[2,32,6,32,32]{4,3,2,1,0:T(8,128)} %fusion.14, bf16[2,32,32,6,64]{4,3,2,1,0:T(8,128)(2,1)} %reshape.72, f32[2,32,6,32,32]{3,4,2,1,0:T(8,128)} %get-tuple-element.6, f32[2,32,6,32]{3,2,1,0:T(8,128)S(1)} %get-tuple-element.5), kind=kOutput, calls=%fused_computation.29 | convolution fusion | flops 53882912 | bytes 6340608 | tf_op jit(solution)/shard_map/bchij,bjchd->bichd/dot_general | solution.py:55
  157.0 5.2 %copy.82 = bf16[2,32,32,6,64]{4,3,2,0,1:T(8,128)(2,1)} copy(bf16[2,32,32,6,64]{4,1,3,2,0:T(8,128)(2,1)} %convert_bitcast_fusion.2) | data formatting | bytes 3145728 | tf_op jit(solution)/shard_map/reshape | solution.py:61
  162.2 6.0 %reshape.81 = bf16[2,32,32,384]{3,2,0,1:T(8,128)(2,1)} reshape(bf16[2,32,32,6,64]{4,3,2,0,1:T(8,128)(2,1)} %copy.82) | data formatting | bytes 3145728 | tf_op jit(solution)/shard_map/reshape | solution.py:61
  168.3 3.7 %all-to-all-start.4 = ((bf16[2,32,32,384]{3,2,0,1:T(8,128)(2,1)}), bf16[2,32,32,384]{3,2,0,1:T(8,128)(2,1)S(1)}, u32[]{:S(2)}, u32[]{:S(2)}) async-start(bf16[2,32,32,384]{3,2,0,1:T(8,128)(2,1)} %reshape.81), calls=%async_computation.4 | async-start | bytes 3145728 | tf_op jit(solution)/shard_map/all_to_all | solution.py:92
  172.0 15.1 %convert_bitcast_fusion.1 = bf16[2,32,32,6,64]{4,1,3,2,0:T(8,128)(2,1)} fusion(f32[2,32,6,32,32]{4,3,2,1,0:T(8,128)} %fusion.14, bf16[2,32,32,6,64]{4,3,2,1,0:T(8,128)(2,1)} %reshape.73, f32[2,32,6,32,32]{3,4,2,1,0:T(8,128)} %get-tuple-element.6, f32[2,32,6,32]{3,2,1,0:T(8,128)} %copy-done.10), kind=kOutput, calls=%fused_computation.28 | convolution fusion | flops 53882912 | bytes 6340608 | tf_op jit(solution)/shard_map/bchij,bichd->bjchd/dot_general | solution.py:58
  187.1 5.3 %copy.84 = bf16[2,32,32,6,64]{4,3,2,0,1:T(8,128)(2,1)} copy(bf16[2,32,32,6,64]{4,1,3,2,0:T(8,128)(2,1)} %convert_bitcast_fusion.1) | data formatting | bytes 3145728 | tf_op jit(solution)/shard_map/reshape | solution.py:61
  192.4 6.1 %reshape.82 = bf16[2,32,32,384]{3,2,0,1:T(8,128)(2,1)} reshape(bf16[2,32,32,6,64]{4,3,2,0,1:T(8,128)(2,1)} %copy.84) | data formatting | bytes 3145728 | tf_op jit(solution)/shard_map/reshape | solution.py:61
  198.4 0.0 all-to-all-done.4
  198.4 4.4 %all-to-all-start.5 = ((bf16[2,32,32,384]{3,2,0,1:T(8,128)(2,1)}), bf16[2,32,32,384]{3,2,0,1:T(8,128)(2,1)}, u32[]{:S(2)}, u32[]{:S(2)}) async-start(bf16[2,32,32,384]{3,2,0,1:T(8,128)(2,1)} %reshape.82), calls=%async_computation.5 | async-start | bytes 3145728 | tf_op jit(solution)/shard_map/all_to_all | solution.py:93
  202.8 6.4 %convert_bitcast_fusion = bf16[2,32,32,6,64]{4,1,3,2,0:T(8,128)(2,1)S(1)} fusion(bf16[2,32,32,6,64]{4,3,2,1,0:T(8,128)(2,1)} %reshape.75, f32[2,32,6,32,32]{3,4,2,1,0:T(8,128)} %get-tuple-element.6, f32[2,32,6,32]{3,2,1,0:T(8,128)} %copy-done.10), kind=kOutput, calls=%fused_computation.25 | convolution fusion | flops 51904512 | bytes 4767744 | tf_op jit(solution)/shard_map/bchij,bichd->bjchd/dot_general | solution.py:47
  209.2 3.3 copy.86
  212.5 6.1 %reshape.83 = bf16[2,32,32,384]{3,2,0,1:T(8,128)(2,1)} reshape(bf16[2,32,32,6,64]{4,3,2,0,1:T(8,128)(2,1)} %copy.86) | data formatting | bytes 3145728 | tf_op jit(solution)/shard_map/reshape | solution.py:61
  218.6 4.4 %all-to-all-done.5 = bf16[2,32,32,384]{3,2,0,1:T(8,128)(2,1)} async-done(((bf16[2,32,32,384]{3,2,0,1:T(8,128)(2,1)}), bf16[2,32,32,384]{3,2,0,1:T(8,128)(2,1)}, u32[]{:S(2)}, u32[]{:S(2)}) %all-to-all-start.5) | async-done | bytes 1572896 | tf_op jit(solution)/shard_map/all_to_all | solution.py:93
  223.0 4.3 %all-to-all-start.6 = ((bf16[2,32,32,384]{3,2,0,1:T(8,128)(2,1)}), bf16[2,32,32,384]{3,2,0,1:T(8,128)(2,1)}, u32[]{:S(2)}, u32[]{:S(2)}) async-start(bf16[2,32,32,384]{3,2,0,1:T(8,128)(2,1)} %reshape.83), calls=%async_computation.6 | async-start | bytes 3145728 | tf_op jit(solution)/shard_map/all_to_all | solution.py:94
  227.3 0.3 reduce-scatter.5.cloned.1.call-start
  227.6 1.4 copy.63
  229.0 2.9 copy.68
  231.9 15.5 %all-to-all-done.6 = bf16[2,32,32,384]{3,2,0,1:T(8,128)(2,1)} async-done(((bf16[2,32,32,384]{3,2,0,1:T(8,128)(2,1)}), bf16[2,32,32,384]{3,2,0,1:T(8,128)(2,1)}, u32[]{:S(2)}, u32[]{:S(2)}) %all-to-all-start.6) | async-done | bytes 1572896 | tf_op jit(solution)/shard_map/all_to_all | solution.py:94
  247.5 1.6 copy.73
  249.1 0.0 copy-start.7
  249.1 1.1 copy-done.7
  250.2 8.0 %convolution_bitcast_fusion = f32[768,1152]{0,1:T(8,128)} fusion(bf16[2,8,128,768]{3,2,1,0:T(8,128)(2,1)} %copy-done.5, bf16[2,8,128,384]{3,2,1,0:T(8,128)(2,1)S(1)} %bitcast.101, bf16[2,8,128,384]{3,2,1,0:T(8,128)(2,1)} %bitcast.99, bf16[2,8,128,384]{3,2,1,0:T(8,128)(2,1)S(1)} %bitcast.97), kind=kOutput, calls=%fused_computation.22 | convolution fusion | flops 3638034432 | bytes 11403264 | tf_op jit(solution)/shard_map/dot_general | solution.py:67
  258.3 0.0 reduce-scatter.5.cloned.1.call-update
  258.3 0.0 reduce-scatter.7.cloned.1.call-start
  258.4 80.2 %reduce-scatter.5.cloned.1.call-done = f32[768,144]{0,1:T(8,128)} async-done(((f32[768,1152]{0,1:T(8,128)}), f32[768,144]{0,1:T(8,128)}) %reduce-scatter.5.cloned.1.call-update) | async-done | bytes 442384 | tf_op jit(solution)/shard_map/reduce_scatter | solution.py:98
  338.6 2.2 copy.88
  340.7 0.0 reduce-scatter.7.cloned.1.call-update
  340.8 0.0 copy-start.2
  340.8 7.1 %fusion.5 = (f32[2,8,128]{2,1,0:T(8,128)S(1)}, f32[2,8,128,768]{3,2,1,0:T(8,128)S(1)}) fusion(bf16[2,8,128,768]{3,2,1,0:T(8,128)(2,1)} %param.4, f32[2,8,128]{2,1,0:T(8,128)S(1)} %add_rsqrt_fusion, bf16[768,1152]{1,0:T(8,128)(2,1)S(1)} %copy-done, bf16[2,8,128,384]{3,2,1,0:T(8,128)(2,1)} %bitcast.102, bf16[2,8,128,384]{3,2,1,0:T(8,128)(2,1)} %bitcast.100, ...), kind=kOutput, calls=%fused_computation.8 | convolution fusion | flops 3644323840 | bytes 15941632 | tf_op jit(solution)/shard_map/dot_general | solution.py:70
  347.9 2.4 fusion.8
  350.4 13.6 %reduce-scatter.7.cloned.1.call-done = f32[192,144]{1,0:T(8,128)} async-done(((f32[768,144]{1,0:T(8,128)}), f32[192,144]{1,0:T(8,128)}) %reduce-scatter.7.cloned.1.call-update) | async-done | bytes 110608
  363.9 1.7 copy.89
  (18 shorter events, 0.0 us)
Async XLA Ops:
  7.2 3.6 copy-start
  7.2 3.0 copy-start.1
  10.7 4.5 %copy-start.5 = (bf16[2,8,128,768]{3,2,1,0:T(8,128)(2,1)}, bf16[2,8,128,768]{3,2,1,0:T(8,128)(2,1)S(1)}, u32[]{:S(2)}) copy-start(bf16[2,8,128,768]{3,2,1,0:T(8,128)(2,1)S(1)} %fusion.4) | copy-start | bytes 9437188
  19.6 24.3 %all-to-all-start = ((bf16[2,8,128,384]{3,1,0,2:T(8,128)(2,1)}), bf16[2,8,128,384]{3,1,0,2:T(8,128)(2,1)S(1)}, u32[]{:S(2)}, u32[]{:S(2)}) async-start(bf16[2,8,128,384]{3,1,0,2:T(8,128)(2,1)} %copy.93), calls=%async_computation | async-start | bytes 3145728 | tf_op jit(solution)/shard_map/all_to_all | solution.py:84
  43.9 24.5 %all-to-all-start.1 = ((bf16[2,8,128,384]{3,1,0,2:T(8,128)(2,1)}), bf16[2,8,128,384]{3,1,0,2:T(8,128)(2,1)}, u32[]{:S(2)}, u32[]{:S(2)}) async-start(bf16[2,8,128,384]{3,1,0,2:T(8,128)(2,1)} %copy.94), calls=%async_computation.1 | async-start | bytes 3145728 | tf_op jit(solution)/shard_map/all_to_all | solution.py:83
  51.7 45.8 %copy-start.9 = (s32[2,32,32]{2,1,0:T(8,128)S(1)}, s32[2,32,32]{2,1,0:T(8,128)}, u32[]{:S(2)}) copy-start(s32[2,32,32]{2,1,0:T(8,128)} %param.6) | copy-start | bytes 24580
  68.4 24.5 %all-to-all-start.2 = ((bf16[2,8,128,384]{3,1,0,2:T(8,128)(2,1)}), bf16[2,8,128,384]{3,1,0,2:T(8,128)(2,1)}, u32[]{:S(2)}, u32[]{:S(2)}) async-start(bf16[2,8,128,384]{3,1,0,2:T(8,128)(2,1)} %copy.95), calls=%async_computation.2 | async-start | bytes 3145728 | tf_op jit(solution)/shard_map/all_to_all | solution.py:85
  92.9 24.7 %all-to-all-start.3 = ((bf16[2,8,128,384]{3,1,0,2:T(8,128)(2,1)}), bf16[2,8,128,384]{3,1,0,2:T(8,128)(2,1)}, u32[]{:S(2)}, u32[]{:S(2)}) async-start(bf16[2,8,128,384]{3,1,0,2:T(8,128)(2,1)} %copy.54), calls=%async_computation.3 | async-start | bytes 3145728 | tf_op jit(solution)/shard_map/all_to_all | solution.py:86
  123.1 7.5 %copy-start.8 = (pred[2,32,32,32]{2,3,1,0:T(8,128)(4,1)S(1)}, pred[2,32,32,32]{2,3,1,0:T(8,128)(4,1)}, u32[]{:S(2)}) copy-start(pred[2,32,32,32]{2,3,1,0:T(8,128)(4,1)} %compare_or_fusion) | copy-start | bytes 196612
  130.7 4.7 %copy-start.3 = (bf16[2,32,32,6,64]{4,3,2,1,0:T(8,128)(2,1)S(1)}, bf16[2,32,32,6,64]{4,3,2,1,0:T(8,128)(2,1)}, u32[]{:S(2)}) copy-start(bf16[2,32,32,6,64]{4,3,2,1,0:T(8,128)(2,1)} %reshape.75) | copy-start | bytes 4718596
  130.7 5.7 %copy-start.4 = (bf16[2,32,32,6,64]{4,3,2,1,0:T(8,128)(2,1)S(1)}, bf16[2,32,32,6,64]{4,3,2,1,0:T(8,128)(2,1)}, u32[]{:S(2)}) copy-start(bf16[2,32,32,6,64]{4,3,2,1,0:T(8,128)(2,1)} %reshape.74) | copy-start | bytes 4718596
  136.4 6.3 %copy-start.10 = (f32[2,32,6,32]{3,2,1,0:T(8,128)}, f32[2,32,6,32]{3,2,1,0:T(8,128)S(1)}, u32[]{:S(2)}) copy-start(f32[2,32,6,32]{3,2,1,0:T(8,128)S(1)} %get-tuple-element.5) | copy-start | bytes 147460
  168.3 30.2 %all-to-all-start.4 = ((bf16[2,32,32,384]{3,2,0,1:T(8,128)(2,1)}), bf16[2,32,32,384]{3,2,0,1:T(8,128)(2,1)S(1)}, u32[]{:S(2)}, u32[]{:S(2)}) async-start(bf16[2,32,32,384]{3,2,0,1:T(8,128)(2,1)} %reshape.81), calls=%async_computation.4 | async-start | bytes 3145728 | tf_op jit(solution)/shard_map/all_to_all | solution.py:92
  198.4 24.5 %all-to-all-start.5 = ((bf16[2,32,32,384]{3,2,0,1:T(8,128)(2,1)}), bf16[2,32,32,384]{3,2,0,1:T(8,128)(2,1)}, u32[]{:S(2)}, u32[]{:S(2)}) async-start(bf16[2,32,32,384]{3,2,0,1:T(8,128)(2,1)} %reshape.82), calls=%async_computation.5 | async-start | bytes 3145728 | tf_op jit(solution)/shard_map/all_to_all | solution.py:93
  223.0 24.5 %all-to-all-start.6 = ((bf16[2,32,32,384]{3,2,0,1:T(8,128)(2,1)}), bf16[2,32,32,384]{3,2,0,1:T(8,128)(2,1)}, u32[]{:S(2)}, u32[]{:S(2)}) async-start(bf16[2,32,32,384]{3,2,0,1:T(8,128)(2,1)} %reshape.83), calls=%async_computation.6 | async-start | bytes 3145728 | tf_op jit(solution)/shard_map/all_to_all | solution.py:94
  227.3 111.3 %reduce-scatter.5.cloned.1.call-start = ((), (), s32[]{:S(2)}) async-start(), calls=%async_computation.9 | async-start | bytes 3981312 | tf_op jit(solution)/shard_map/reduce_scatter | solution.py:98
  229.0 21.3 %copy-start.6 = (bf16[2,8,4,32,384]{4,3,2,1,0:T(8,128)(2,1)S(1)}, bf16[2,8,4,32,384]{4,3,2,1,0:T(8,128)(2,1)}, u32[]{:S(2)}) copy-start(bf16[2,8,4,32,384]{4,3,2,1,0:T(8,128)(2,1)} %copy.63) | copy-start | bytes 4718596
  249.1 1.1 copy-start.7
  258.3 105.6 %reduce-scatter.7.cloned.1.call-start = ((), (), s32[]{:S(2)}) async-start(), calls=%async_computation.10 | async-start | bytes 983040
  340.8 7.2 %copy-start.2 = (bf16[2,8,128,768]{3,2,1,0:T(8,128)(2,1)S(1)}, bf16[2,8,128,768]{3,2,1,0:T(8,128)(2,1)}, u32[]{:S(2)}) copy-start(bf16[2,8,128,768]{3,2,1,0:T(8,128)(2,1)} %param.4) | copy-start | bytes 9437188
Sparse Core Ops, SparseCore 0:
  258.4 80.1 reduce-scatter.4
  341.1 22.7 reduce-scatter.6
where the time goes:
time: 380 us; the launch traced here: 373 us
  waiting for transfers between devices  164 us (43%)
  local copies, waits for them, and re-layouts  82.9 us (22%)
  matrix products  69.3 us (18%)
  starting transfers between devices  30.2 us (8%)
  between operations  14.5 us (4%)
  other arithmetic  11.5 us (3%)
    reduce_scatter x1, waiting for transfers between devices, body(): shared = lax.psum_scatter(partial_w, 'dp', scatter_dimension=1, tiled=True)  80.2 us
    unnamed x28, local copies, waits for them, and re-layouts  18.8 us
    all_to_all x1, waiting for transfers between devices, body(): lax.all_to_all(value_rows, 'band', split_axis=2, concat_axis=1, tiled=True)  16.7 us
    all_to_all x1, waiting for transfers between devices, body(): lax.all_to_all(query_rows, 'band', split_axis=2, concat_axis=1, tiled=True)  16.7 us
    all_to_all x1, waiting for transfers between devices, body(): lax.all_to_all(key_rows, 'band', split_axis=2, concat_axis=1, tiled=True)  16.6 us
    all_to_all x1, waiting for transfers between devices, body(): lax.all_to_all(value_grad, 'band', split_axis=1, concat_axis=2, tiled=True)  15.5 us
    dot_general x1, matrix products, attend_back(): jnp.einsum('bchij,bichd->bjchd', score_low, query_five, preferred_element...  15.1 us
    dot_general x1, matrix products, attend_back(): jnp.einsum('bchij,bjchd->bichd', score_low, key_five, preferred_element_t...  14.3 us
  transfers between devices with their start and end apart: 9, of which 8 were waited for; matrix products, arithmetic and copies ran while one was open for 23% of the time, Pallas kernels for 0%

commit v1 on v0

--- a/solution.py
+++ b/solution.py
@@ -1,13 +1,227 @@
+import functools
+
 import jax
 import jax.numpy as jnp
 from jax import lax
+from jax.experimental import pallas as pl
+from jax.experimental.pallas import tpu as pltpu
 from jax.sharding import PartitionSpec as P
 
 HD = 64
-
-
 SCALE = 0.125
 EPSILON = 1e-06
+LOW = 4
+HIGH = 3
+BAND = 8
+SLOTS = 1 + LOW + BAND + HIGH
+SUB = 8
+STEP = 16
+CELLS = SLOTS * SUB
+F32 = jnp.float32
+BF16 = jnp.bfloat16
+
+
+def dot(a, b, ca, cb):
+    return lax.dot_general(a, b, (((ca,), (cb,)), ((), ())), preferred_element_type=F32)
+
+
+def split_heads(a):
+    left = lax.broadcasted_iota(jnp.int32, a.shape, 1) < HD
+    zero = jnp.zeros_like(a)
+    return jnp.concatenate((jnp.where(left, a, zero), jnp.where(left, zero, a)), axis=0)
+
+
+def kernel(first, *refs):
+    if first:
+        code, hx, lx, ox, ux, lg, og, ug, w, out_h, out_l, out_o, out_u, wg, mixed, grads = refs
+    else:
+        code, hx, lx, ox, ux, lg, og, ug, w, wg_in, out_h, out_l, out_o, out_u, wg, mixed, grads = refs
+    width = og.shape[-1]
+
+    def flat(parts):
+        whole = jnp.concatenate(parts, axis=0).astype(F32)
+        return jnp.concatenate(
+            [whole[:, s : s + SUB].reshape(CELLS, whole.shape[-1]) for s in range(0, STEP, SUB)], axis=0
+        )
+
+    states = flat((hx[0], lx[0], ox[0], ux[0]))
+    inverse = lax.rsqrt(jnp.mean(states * states, axis=-1, keepdims=True) + EPSILON)
+    scaled = states * inverse
+    normed = scaled.astype(BF16)
+    mixed[...] = dot(normed, w[...], 1, 0).astype(BF16)
+    cotangent = flat((jnp.zeros((1, STEP, width), BF16), lg[0], og[0], ug[0])).astype(BF16)
+
+    for s in range(STEP // SUB):
+        rows = slice(s * CELLS, (s + 1) * CELLS)
+        query_code = code[0, 0, s : s + 1, :]
+        key_code = jnp.broadcast_to(code[0, 0, s + 2 : s + 3, :], (CELLS, CELLS)).T
+        query_column = query_code >> 3
+        at = lax.broadcasted_iota(jnp.int32, (CELLS, CELLS), 0)
+        visible = (key_code == query_code) | (at == query_column)
+        bias = jnp.where(visible, 0.0, -1e30).astype(F32)
+        for p in range(width // 128):
+            lanes = slice(128 * p, 128 * p + 128)
+            query = mixed[rows, lanes] * jnp.asarray(SCALE, BF16)
+            key = mixed[rows, width + 128 * p : width + 128 * p + 128]
+            value = mixed[rows, 2 * width + 128 * p : 2 * width + 128 * p + 128]
+            grad = cotangent[rows, lanes]
+            scores = dot(split_heads(key), query, 1, 1).reshape(2, CELLS, CELLS) + bias[None]
+            peak = jnp.maximum(jnp.max(scores, axis=1, keepdims=True), -1e29)
+            expsc = jnp.exp(scores - peak)
+            total = jnp.maximum(jnp.sum(expsc, axis=1, keepdims=True), 1.0)
+            probs = expsc * (1.0 / total)
+            prob_grad = dot(split_heads(value), grad, 1, 1).reshape(2, CELLS, CELLS)
+            delta = jnp.sum(probs * prob_grad, axis=1, keepdims=True)
+            score_low = (probs * (prob_grad - delta)).astype(BF16)
+            probs_low = probs.astype(BF16)
+            value_grad = dot(
+                jnp.concatenate((probs_low[0], probs_low[1]), axis=1), split_heads(grad), 1, 0
+            )
+            key_grad = dot(
+                jnp.concatenate((score_low[0], score_low[1]), axis=1), split_heads(query), 1, 0
+            )
+            query_grad = dot(
+                score_low.reshape(2 * CELLS, CELLS), split_heads(key * jnp.asarray(SCALE, BF16)), 0, 0
+            )
+            grads[rows, lanes] = query_grad.astype(BF16)
+            grads[rows, width + 128 * p : width + 128 * p + 128] = key_grad.astype(BF16)
+            grads[rows, 2 * width + 128 * p : 2 * width + 128 * p + 128] = value_grad.astype(BF16)
+
+    normed_grad = dot(grads[...], w[...], 1, 1)
+    coupling = jnp.mean(normed_grad * scaled, axis=-1, keepdims=True)
+    result = inverse * (normed_grad - scaled * coupling)
+    parts = [result[s * CELLS : (s + 1) * CELLS].reshape(SLOTS, SUB, -1) for s in range(STEP // SUB)]
+    result = jnp.concatenate(parts, axis=1).astype(BF16)
+    out_h[0] = result[:1]
+    out_l[0] = result[1 : 1 + LOW]
+    out_o[0] = result[1 + LOW : 1 + LOW + BAND]
+    out_u[0] = result[1 + LOW + BAND :]
+
+    term = dot(normed, grads[...], 0, 0)
+
+    @pl.when(pl.program_id(0) == 0)
+    def _():
+        wg[...] = term if first else wg_in[...] + term
+
+    @pl.when(pl.program_id(0) != 0)
+    def _():
+        wg[...] += term
+
+
+def attend(code, states, cots, weights, earlier):
+    cols, wide = states[2].shape[2:]
+    width = cots[1].shape[-1]
+
+    def block(rows, features):
+        return pl.BlockSpec((1, rows, STEP, features), lambda i: (0, 0, i, 0))
+
+    whole = lambda shape: pl.BlockSpec(shape, lambda i: (0,) * len(shape))
+    in_specs = [pl.BlockSpec((1, 1, 2 * STEP // SUB, CELLS), lambda i: (0, i, 0, 0))]
+    in_specs += [block(r, wide) for r in (1, LOW, BAND, HIGH)]
+    in_specs += [block(r, width) for r in (LOW, BAND, HIGH)]
+    in_specs += [whole(weights.shape)]
+    operands = [code, *states, *cots, weights]
+    aliases = {}
+    if earlier is not None:
+        aliases = {len(operands): 4}
+        in_specs.append(whole(weights.shape))
+        operands.append(earlier)
+    out_shape = [jax.ShapeDtypeStruct((1, r, cols, wide), BF16) for r in (1, LOW, BAND, HIGH)]
+    out_shape.append(jax.ShapeDtypeStruct(weights.shape, F32))
+    many = SLOTS * cols
+    return pl.pallas_call(
+        functools.partial(kernel, earlier is None),
+        grid=(cols // STEP,),
+        in_specs=in_specs,
+        out_specs=[block(r, wide) for r in (1, LOW, BAND, HIGH)] + [whole(weights.shape)],
+        out_shape=out_shape,
+        scratch_shapes=[
+            pltpu.VMEM((SLOTS * STEP, 3 * width), BF16),
+            pltpu.VMEM((SLOTS * STEP, 3 * width), BF16),
+        ],
+        input_output_aliases=aliases,
+        compiler_params=pltpu.CompilerParams(vmem_limit_bytes=48 * 1024 * 1024),
+        cost_estimate=pl.CostEstimate(
+            flops=6 * many * wide * 3 * width + 10 * many * 128 * width * 2,
+            bytes_accessed=many * (4 * wide + 2 * width) + 8 * wide * 3 * width,
+            transcendentals=many * 128 * 6,
+        ),
+    )(*operands)
+
+
+def group_codes(group_ids):
+    rows = group_ids.shape[-1]
+    same = group_ids[:, :, :, None] == group_ids[:, :, None, :]
+    at = jnp.arange(rows)
+    before = jnp.sum(same & (at[None, :] < at[:, None]), axis=-1)
+    after = jnp.sum(same & (at[None, :] > at[:, None]), axis=-1)
+    start, end = at - before, at + after
+    first, last = start // BAND, end // BAND
+    border = last * BAND
+    owner = jnp.where((first != last) & (border - start > end + 1 - border), first, last)
+    return (group_ids + 8 * owner).astype(jnp.int32)
+
+
+def slot_codes(codes, band):
+    tables, cols, rows = codes.shape
+    padded = jnp.pad(codes, ((0, 0), (0, 0), (LOW, HIGH)), constant_values=-8)
+    near = lax.dynamic_slice_in_dim(padded, band * BAND, LOW + BAND + HIGH, axis=2)
+    row = band * BAND - LOW + jnp.arange(LOW + BAND + HIGH)
+    alive = (near >> 3) == band
+    mark = (jnp.arange(cols) % SUB)[None, :, None] * 8 + (near & 7)
+    query = jnp.where(alive, mark, -1)
+    key = jnp.where(alive & (row != 0), mark, -2)
+
+    def order(values, header):
+        values = jnp.pad(values, ((0, 0), (0, 0), (1, 0)), constant_values=header)
+        values = values.reshape(tables, cols // STEP, STEP // SUB, SUB, SLOTS)
+        return values.transpose(0, 1, 2, 4, 3).reshape(tables, cols // STEP, STEP // SUB, CELLS)
+
+    return jnp.concatenate((order(query, -1), order(key, -2)), axis=2).astype(jnp.int32)
+
+
+def halo_body(cell_states, head_grads, group_ids, proj_weights):
+    bands = lax.axis_size("band")
+    band = lax.axis_index("band")
+    tables = cell_states.shape[0]
+    up = [(i, i + 1) for i in range(bands - 1)]
+    down = [(i + 1, i) for i in range(bands - 1)]
+    send = lambda a, pairs: lax.ppermute(a, "band", pairs)
+    far = [(0, bands // 2)]
+    near = [(0, 1), (bands // 2, bands // 2 + 1)]
+    back = lambda pairs: [(b, a) for a, b in pairs]
+
+    codes = lax.all_gather(group_codes(group_ids), "band", axis=1, tiled=True)
+    codes = slot_codes(codes, band)
+    weight_sum = None
+    outputs = []
+    for t in range(tables):
+        states, cots = cell_states[t : t + 1], head_grads[t : t + 1]
+        mine = states[:, :1]
+        mine = jnp.where(band == bands // 2, send(mine, far), mine)
+        header = jnp.where(band % 2 == 1, send(mine, near), mine)
+        pieces = (
+            header,
+            send(states[:, BAND - LOW :], up),
+            states,
+            send(states[:, :HIGH], down),
+        )
+        cot_pieces = (send(cots[:, BAND - LOW :], up), cots, send(cots[:, :HIGH], down))
+        out_h, out_l, out_o, out_u, weight_sum = attend(
+            codes[t : t + 1], pieces, cot_pieces, proj_weights, weight_sum
+        )
+        from_high = send(out_l, down).astype(F32)
+        from_low = send(out_u, up).astype(F32)
+        head = out_h.astype(F32) + send(out_h, back(near)).astype(F32)
+        head = head + send(head.astype(BF16), back(far)).astype(F32)
+        head = jnp.where(band == 0, head, 0.0)
+        whole = out_o.astype(F32)
+        pad = lambda a, lo: jnp.pad(a, ((0, 0), (lo, BAND - lo - a.shape[1]), (0, 0), (0, 0)))
+        whole = whole + pad(from_high, BAND - LOW) + pad(from_low, 0) + pad(head, 0)
+        outputs.append(whole.astype(BF16))
+    shared = lax.psum_scatter(weight_sum, "band", scatter_dimension=0, tiled=True)
+    weight_grad = lax.psum_scatter(shared, "dp", scatter_dimension=1, tiled=True)
+    return (jnp.concatenate(outputs, axis=0), weight_grad)
 
 
 def normalize(states):
@@ -76,7 +290,7 @@
     return (partial_w, state_grad)
 
 
-def body(cell_states, head_grads, group_ids, proj_weights):
+def exchange_body(cell_states, head_grads, group_ids, proj_weights):
     scaled, inverse, normed = normalize(cell_states)
     query_rows, key_rows, value_rows = project(normed, proj_weights)
     query_cols, key_cols, value_cols, grad_cols = (
@@ -98,6 +312,12 @@
     shared = lax.psum_scatter(partial_w, "dp", scatter_dimension=1, tiled=True)
     weight_grad = lax.psum_scatter(shared, "band", scatter_dimension=0, tiled=True)
     return (input_grad, weight_grad)
+
+
+def body(cell_states, head_grads, group_ids, proj_weights):
+    halo = cell_states.shape[1] == BAND and lax.axis_size("band") == 4
+    form = halo_body if halo else exchange_body
+    return form(cell_states, head_grads, group_ids, proj_weights)
 
 
 def solution(mesh):

time: 380 us -> 267 us (0.70); the launches traced: 373 us -> 266 us
  waiting for transfers between devices: 164 us -> 83.8 us
  Pallas kernels: 0 us -> 72.8 us
  matrix products: 69.3 us -> 0 us
  local copies, waits for them, and re-layouts: 82.9 us -> 23.6 us
  starting transfers between devices: 30.2 us -> 50.1 us
  blocking collectives: 0 us -> 5.56 us
  other arithmetic: 11.5 us -> 15.5 us
    pallas_call x0 -> x2, Pallas kernels: none -> 72.8 us  [attend(): pl.pallas_call(functools.partial(kernel, earlier is None), grid=(cols //...]
    all_to_all x7 -> x0, waiting for transfers between devices: 70.5 us -> none  [the longest x1 16.7 us: body(): lax.all_to_all(value_rows, 'band', split_axis=2, concat_axis=1, tiled=True)]
    dot_general x8 -> x0, matrix products: 69.3 us -> none  [the longest x1 15.1 us: attend_back(): jnp.einsum('bchij,bichd->bjchd', score_low, query_five, preferred_element...]
    reduce_scatter x1, waiting for transfers between devices: 80.2 us -> 28.9 us  [halo_body(): lax.psum_scatter(weight_sum, 'band', scatter_dimension=0, tiled=True)]
    ppermute x0 -> x20, starting transfers between devices: none -> 50 us  [halo_body(): send = lambda a, pairs: lax.ppermute(a, 'band', pairs)]
    reshape x10 -> x6, local copies, waits for them, and re-layouts: 49.1 us -> 0.59 us  [the longest x4 0.32 us: order(): values.transpose(0, 1, 2, 4, 3)]
    all_to_all x7 -> x0, starting transfers between devices: 29.9 us -> none  [the longest x1 4.6 us: body(): lax.all_to_all(head_grads, 'band', split_axis=2, concat_axis=1, tiled=True)]
    unnamed x3, waiting for transfers between devices: 13.6 us -> 36.5 us
  transfers between devices with their start and end apart: 9 -> 22, of which waited for: 8 -> 7; matrix products, arithmetic and copies ran while one was open for 23% -> 11% of each run, Pallas kernels for 0% -> 13%
where the time goes in v1:
time: 267 us; the launch traced here: 266 us
  waiting for transfers between devices  83.8 us (31%)
  Pallas kernels  72.8 us (27%)
  starting transfers between devices  50.1 us (19%)
  local copies, waits for them, and re-layouts  23.6 us (9%)
  other arithmetic  15.5 us (6%)
  between operations  14.5 us (5%)
  blocking collectives  5.56 us (2%)
    pallas_call x2, Pallas kernels, attend(): pl.pallas_call(functools.partial(kernel, earlier is None), grid=(cols //...  72.8 us
    ppermute x20, starting transfers between devices, halo_body(): send = lambda a, pairs: lax.ppermute(a, 'band', pairs)  50 us
    unnamed x3, waiting for transfers between devices  36.5 us
    reduce_scatter x1, waiting for transfers between devices, halo_body(): lax.psum_scatter(weight_sum, 'band', scatter_dimension=0, tiled=True)  28.9 us
    ppermute x20, waiting for transfers between devices, halo_body(): send = lambda a, pairs: lax.ppermute(a, 'band', pairs)  18.4 us
    unnamed x29, local copies, waits for them, and re-layouts  11.4 us
    all_gather x1, blocking collectives, halo_body(): codes = lax.all_gather(group_codes(group_ids), 'band', axis=1, tiled=True)  5.56 us
  transfers between devices with their start and end apart: 22, of which 7 were waited for; matrix products, arithmetic and copies ran while one was open for 11% of the time, Pallas kernels for 13%

profile of v1, /device:TPU:0, one launch (start us, length us, event | category | flops | bytes accessed | tf_op | source)
XLA Modules:
  0.0 265.9 jit_solution(10138434878294255141)
XLA Ops:
  7.2 1.1 slice.59
  8.3 4.9 %collective-permute-start = (bf16[1,1,128,768]{3,2,1,0:T(8,128)(2,1)S(1)}, bf16[1,1,128,768]{3,2,1,0:T(8,128)(2,1)S(1)}, u32[]{:S(2)}, u32[]{:S(2)}) collective-permute-start(bf16[1,1,128,768]{3,2,1,0:T(8,128)(2,1)S(1)} %slice.59), channel_id=1, source_target_pairs={{0,2},{4,6},{8,10},{12,14},{16,18},{20,22},{24,26},{28,30}} | collective-permute-start | bytes 589832 | tf_op jit(solution)/shard_map/ppermute | solution.py:189
  13.2 1.9 fusion.13
  15.1 1.3 collective-permute-start.5
  16.4 2.1 fusion.15
  18.5 3.2 %collective-permute-start.4 = (bf16[1,4,128,384]{3,2,1,0:T(8,128)(2,1)}, bf16[1,4,128,384]{3,2,1,0:T(8,128)(2,1)S(1)}, u32[]{:S(2)}, u32[]{:S(2)}) collective-permute-start(bf16[1,4,128,384]{3,2,1,0:T(8,128)(2,1)} %get-tuple-element.46), channel_id=1, source_target_pairs={{0,1},{1,2},{2,3},{4,5},{5,6},{6,7},{8,9},{9,10},{10,11},{12,13},{... | collective-permute-start | bytes 1179656 | tf_op jit(solution)/shard_map/ppermute | solution.py:189
  21.7 1.1 fusion.10
  22.8 1.3 collective-permute-start.3
  24.1 1.3 fusion.12
  25.4 3.1 %collective-permute-start.2 = (bf16[1,4,128,768]{3,2,1,0:T(8,128)(2,1)}, bf16[1,4,128,768]{3,2,1,0:T(8,128)(2,1)S(1)}, u32[]{:S(2)}, u32[]{:S(2)}) collective-permute-start(bf16[1,4,128,768]{3,2,1,0:T(8,128)(2,1)} %get-tuple-element.38), channel_id=1, source_target_pairs={{0,1},{1,2},{2,3},{4,5},{5,6},{6,7},{8,9},{9,10},{10,11},{12,13},{... | collective-permute-start | bytes 2359304 | tf_op jit(solution)/shard_map/ppermute | solution.py:189
  28.5 1.1 fusion.14
  29.6 1.9 fusion.11
  31.5 2.7 %convert_reduce_fusion = (s32[2,32,32]{2,1,0:T(8,128)S(1)}, s32[2,32,32]{2,1,0:T(8,128)S(1)}) fusion(s32[2,32,32]{2,1,0:T(8,128)S(1)} %copy-done.13, pred[32,32]{1,0:T(8,128)(4,1)S(1)} %get-tuple-element.50, pred[32,32]{1,0:T(8,128)(4,1)S(1)} %get-tuple-element.51), kind=kLoop, calls=%fused_computation.5 | loop fusion | flops 454656 | bytes 26624 | tf_op jit(solution)/shard_map/reduce_sum | solution.py:157
  34.3 5.6 %all_gather.3 = s32[2,128,32]{2,1,0:T(8,128)S(1)} all-gather(s32[2,32,32]{2,1,0:T(8,128)S(1)} %multiply_add_fusion), channel_id=1, replica_groups=mesh['dp'=8,'band'=4] {'band'}, dimensions={1}, use_global_device_ids=true | all-gather | bytes 40960 | tf_op jit(solution)/shard_map/all_gather | solution.py:194
  39.9 0.8 fusion.2
  40.7 1.7 broadcast_select_fusion.1
  42.4 5.1 %collective-permute-start.10 = (bf16[1,1,128,768]{3,2,1,0:T(8,128)(2,1)}, bf16[1,1,128,768]{3,2,1,0:T(8,128)(2,1)}, u32[]{:S(2)}, u32[]{:S(2)}) collective-permute-start(bf16[1,1,128,768]{3,2,1,0:T(8,128)(2,1)} %get-tuple-element.41), channel_id=1, source_target_pairs={{0,2},{4,6},{8,10},{12,14},{16,18},{20,22},{24,26},{28,30}} | collective-permute-start | bytes 589832 | tf_op jit(solution)/shard_map/ppermute | solution.py:189
  47.5 0.1 and_select_fusion
  47.7 0.1 copy.21
  47.9 0.1 reshape.61
  48.0 1.0 pad.45
  49.0 0.1 copy.20
  49.2 0.1 reshape.59
  49.4 0.9 collective-permute-done.10
  50.3 1.3 collective-permute-start.1
  51.6 1.0 broadcast_select_fusion
  52.6 2.3 collective-permute-start.11
  54.9 1.0 collective-permute-done.11
  55.9 1.3 collective-permute-start.15
  57.3 0.7 copy-done.9
  58.0 3.0 %collective-permute-start.14 = (bf16[1,4,128,384]{3,2,1,0:T(8,128)(2,1)}, bf16[1,4,128,384]{3,2,1,0:T(8,128)(2,1)S(1)}, u32[]{:S(2)}, u32[]{:S(2)}) collective-permute-start(bf16[1,4,128,384]{3,2,1,0:T(8,128)(2,1)} %get-tuple-element.47), channel_id=1, source_target_pairs={{0,1},{1,2},{2,3},{4,5},{5,6},{6,7},{8,9},{9,10},{10,11},{12,13},{... | collective-permute-start | bytes 1179656 | tf_op jit(solution)/shard_map/ppermute | solution.py:189
  61.1 0.8 copy-done.7
  61.8 1.3 collective-permute-start.13
  63.1 0.8 copy-done.3
  63.9 4.8 %collective-permute-start.12 = (bf16[1,4,128,768]{3,2,1,0:T(8,128)(2,1)}, bf16[1,4,128,768]{3,2,1,0:T(8,128)(2,1)S(1)}, u32[]{:S(2)}, u32[]{:S(2)}) collective-permute-start(bf16[1,4,128,768]{3,2,1,0:T(8,128)(2,1)} %get-tuple-element.39), channel_id=1, source_target_pairs={{0,1},{1,2},{2,3},{4,5},{5,6},{6,7},{8,9},{9,10},{10,11},{12,13},{... | collective-permute-start | bytes 2359304 | tf_op jit(solution)/shard_map/ppermute | solution.py:189
  68.8 1.1 copy-done.4
  69.8 1.0 copy-done.8
  70.8 1.0 copy-done.10
  71.8 35.8 %shard_map.59 = (bf16[1,1,128,768]{3,2,1,0:T(8,128)(2,1)S(1)}, bf16[1,4,128,768]{3,2,1,0:T(8,128)(2,1)S(1)}, bf16[1,8,128,768]{3,2,1,0:T(8,128)(2,1)S(1)}, bf16[...) custom-call(s32[1,8,4,128]{3,2,1,0:T(4,128)S(1)} %get-tuple-element.48.refs_0_, ...), custom_call_target="tpu_custom_call" | custom-call | flops 12884901888 | bytes 14942208 | tf_op jit(solution)/shard_map/pallas_call | solution.py:132
  107.6 0.9 copy-done.1
  108.5 0.9 copy-done.5
  109.4 37.0 %shard_map.60 = (bf16[1,1,128,768]{3,2,1,0:T(8,128)(2,1)S(1)}, bf16[1,4,128,768]{3,2,1,0:T(8,128)(2,1)S(1)}, bf16[1,8,128,768]{3,2,1,0:T(8,128)(2,1)S(1)}, bf16[...) custom-call(s32[1,8,4,128]{3,2,1,0:T(4,128)S(1)} %get-tuple-element.49.refs_0_, ...), custom_call_target="tpu_custom_call", output_to_operand_aliasing={{4}: (9, {})} | custom-call | flops 12884901888 | bytes 14942208 | tf_op jit(solution)/shard_map/pallas_call | solution.py:132
  146.4 0.9 copy-done.2
  147.2 0.9 copy-done.6
  148.2 1.3 collective-permute-start.8
  149.5 5.1 %collective-permute-start.7 = (bf16[1,3,128,768]{3,2,1,0:T(8,128)(2,1)}, bf16[1,3,128,768]{3,2,1,0:T(8,128)(2,1)}, u32[]{:S(2)}, u32[]{:S(2)}) collective-permute-start(bf16[1,3,128,768]{3,2,1,0:T(8,128)(2,1)} %copy-done.5), channel_id=1, source_target_pairs={{0,1},{1,2},{2,3},{4,5},{5,6},{6,7},{8,9},{9,10},{10,11},{12,13},{... | collective-permute-start | bytes 1769480 | tf_op jit(solution)/shard_map/ppermute | solution.py:189
  154.6 1.3 collective-permute-start.6
  155.9 1.3 collective-permute-start.18
  157.2 4.5 %collective-permute-start.17 = (bf16[1,3,128,768]{3,2,1,0:T(8,128)(2,1)}, bf16[1,3,128,768]{3,2,1,0:T(8,128)(2,1)}, u32[]{:S(2)}, u32[]{:S(2)}) collective-permute-start(bf16[1,3,128,768]{3,2,1,0:T(8,128)(2,1)} %copy-done.6), channel_id=1, source_target_pairs={{0,1},{1,2},{2,3},{4,5},{5,6},{6,7},{8,9},{9,10},{10,11},{12,13},{... | collective-permute-start | bytes 1769480 | tf_op jit(solution)/shard_map/ppermute | solution.py:189
  161.7 28.9 %reduce-scatter.5.cloned.1.call-done = f32[192,1152]{1,0:T(8,128)} async-done(((f32[768,1152]{1,0:T(8,128)}), f32[192,1152]{1,0:T(8,128)}) %reduce-scatter.5.cloned.1.call-update) | async-done | bytes 884752 | tf_op jit(solution)/shard_map/reduce_scatter | solution.py:222
  190.6 2.6 copy.25
  193.2 1.3 collective-permute-start.16
  194.5 1.0 fusion
  195.5 1.3 collective-permute-start.9
  196.8 1.0 fusion.1
  197.8 11.1 %collective-permute-done.9 = bf16[1,1,128,768]{3,2,1,0:T(8,128)(2,1)S(1)} collective-permute-done((bf16[1,1,128,768]{3,2,1,0:T(8,128)(2,1)S(1)}, bf16[1,1,128,768]{3,2,1,0:T(8,128)(2,1)S(1)}, u32[]{:S(2)}, u32[]{:S(2)}) %collective-permute-start.9) | collective-permute-done | bytes 196640 | tf_op jit(solution)/shard_map/ppermute | solution.py:189
  208.9 1.3 collective-permute-start.19
  210.1 1.0 add_select_fusion.1
  211.2 5.2 %collective-permute-done.19 = bf16[1,1,128,768]{3,2,1,0:T(8,128)(2,1)S(1)} collective-permute-done((bf16[1,1,128,768]{3,2,1,0:T(8,128)(2,1)S(1)}, bf16[1,1,128,768]{3,2,1,0:T(8,128)(2,1)S(1)}, u32[]{:S(2)}, u32[]{:S(2)}) %collective-permute-start.19) | collective-permute-done | bytes 196640 | tf_op jit(solution)/shard_map/ppermute | solution.py:189
  216.4 1.0 add_select_fusion
  217.4 1.7 add_convert_fusion.1
  219.1 1.5 add_convert_fusion
  220.6 1.9 pad_maximum_fusion
  222.5 36.5 %reduce-scatter.7.cloned.1.call-done = f32[144,192]{1,0:T(8,128)} async-done(((f32[1152,192]{1,0:T(8,128)}), f32[144,192]{1,0:T(8,128)}) %reduce-scatter.7.cloned.1.call-update) | async-done | bytes 110608
  (48 shorter events, 0.5 us)
Async XLA Ops:
  7.2 183.4 %reduce-scatter.5.cloned.1.call-start = ((), (), s32[]{:S(2)}) async-start(), calls=%async_computation.2 | async-start | bytes 4423680 | tf_op jit(solution)/shard_map/reduce_scatter | solution.py:222
  7.2 14.5 %copy-start.11 = (bf16[2,8,128,768]{3,2,1,0:T(8,128)(2,1)S(1)}, bf16[2,8,128,768]{3,2,1,0:T(8,128)(2,1)}, u32[]{:S(2)}) copy-start(bf16[2,8,128,768]{3,2,1,0:T(8,128)(2,1)} %param.4) | copy-start | bytes 9437188
  8.3 32.4 %collective-permute-start = (bf16[1,1,128,768]{3,2,1,0:T(8,128)(2,1)S(1)}, bf16[1,1,128,768]{3,2,1,0:T(8,128)(2,1)S(1)}, u32[]{:S(2)}, u32[]{:S(2)}) collective-permute-start(bf16[1,1,128,768]{3,2,1,0:T(8,128)(2,1)S(1)} %slice.59), channel_id=1, source_target_pairs={{0,2},{4,6},{8,10},{12,14},{16,18},{20,22},{24,26},{28,30}} | collective-permute-start | bytes 589832 | tf_op jit(solution)/shard_map/ppermute | solution.py:189
  15.1 42.2 %collective-permute-start.5 = (bf16[1,3,128,384]{3,2,1,0:T(8,128)(2,1)}, bf16[1,3,128,384]{3,2,1,0:T(8,128)(2,1)S(1)}, u32[]{:S(2)}, u32[]{:S(2)}) collective-permute-start(bf16[1,3,128,384]{3,2,1,0:T(8,128)(2,1)} %get-tuple-element.42), channel_id=1, source_target_pairs={{1,0},{2,1},{3,2},{5,4},{6,5},{7,6},{9,8},{10,9},{11,10},{13,12},{... | collective-permute-start | bytes 884744 | tf_op jit(solution)/shard_map/ppermute | solution.py:189
  18.5 10.0 %copy-start.12 = (bf16[2,8,128,384]{3,2,1,0:T(8,128)(2,1)S(1)}, bf16[2,8,128,384]{3,2,1,0:T(8,128)(2,1)}, u32[]{:S(2)}) copy-start(bf16[2,8,128,384]{3,2,1,0:T(8,128)(2,1)} %param.5) | copy-start | bytes 4718596
  18.5 42.5 %collective-permute-start.4 = (bf16[1,4,128,384]{3,2,1,0:T(8,128)(2,1)}, bf16[1,4,128,384]{3,2,1,0:T(8,128)(2,1)S(1)}, u32[]{:S(2)}, u32[]{:S(2)}) collective-permute-start(bf16[1,4,128,384]{3,2,1,0:T(8,128)(2,1)} %get-tuple-element.46), channel_id=1, source_target_pairs={{0,1},{1,2},{2,3},{4,5},{5,6},{6,7},{8,9},{9,10},{10,11},{12,13},{... | collective-permute-start | bytes 1179656 | tf_op jit(solution)/shard_map/ppermute | solution.py:189
  22.8 40.3 %collective-permute-start.3 = (bf16[1,3,128,768]{3,2,1,0:T(8,128)(2,1)}, bf16[1,3,128,768]{3,2,1,0:T(8,128)(2,1)S(1)}, u32[]{:S(2)}, u32[]{:S(2)}) collective-permute-start(bf16[1,3,128,768]{3,2,1,0:T(8,128)(2,1)} %get-tuple-element.34), channel_id=1, source_target_pairs={{1,0},{2,1},{3,2},{5,4},{6,5},{7,6},{9,8},{10,9},{11,10},{13,12},{... | collective-permute-start | bytes 1769480 | tf_op jit(solution)/shard_map/ppermute | solution.py:189
  25.4 43.4 %collective-permute-start.2 = (bf16[1,4,128,768]{3,2,1,0:T(8,128)(2,1)}, bf16[1,4,128,768]{3,2,1,0:T(8,128)(2,1)S(1)}, u32[]{:S(2)}, u32[]{:S(2)}) collective-permute-start(bf16[1,4,128,768]{3,2,1,0:T(8,128)(2,1)} %get-tuple-element.38), channel_id=1, source_target_pairs={{0,1},{1,2},{2,3},{4,5},{5,6},{6,7},{8,9},{9,10},{10,11},{12,13},{... | collective-permute-start | bytes 2359304 | tf_op jit(solution)/shard_map/ppermute | solution.py:189
  29.6 1.9 copy-start.13
  42.4 7.9 %collective-permute-start.10 = (bf16[1,1,128,768]{3,2,1,0:T(8,128)(2,1)}, bf16[1,1,128,768]{3,2,1,0:T(8,128)(2,1)}, u32[]{:S(2)}, u32[]{:S(2)}) collective-permute-start(bf16[1,1,128,768]{3,2,1,0:T(8,128)(2,1)} %get-tuple-element.41), channel_id=1, source_target_pairs={{0,2},{4,6},{8,10},{12,14},{16,18},{20,22},{24,26},{28,30}} | collective-permute-start | bytes 589832 | tf_op jit(solution)/shard_map/ppermute | solution.py:189
  50.3 2.3 collective-permute-start.1
  52.6 3.3 %collective-permute-start.11 = (bf16[1,1,128,768]{3,2,1,0:T(8,128)(2,1)S(1)}, bf16[1,1,128,768]{3,2,1,0:T(8,128)(2,1)S(1)}, u32[]{:S(2)}, u32[]{:S(2)}) collective-permute-start(bf16[1,1,128,768]{3,2,1,0:T(8,128)(2,1)S(1)} %broadcast_select_fusion), channel_id=1, source_target_pairs={{0,1},{2,3},{4,5},{6,7},{8,9},{10,11},{12,13},{14,15},{16,17},{18,... | collective-permute-start | bytes 589832 | tf_op jit(solution)/shard_map/ppermute | solution.py:189
  55.9 53.4 %collective-permute-start.15 = (bf16[1,3,128,384]{3,2,1,0:T(8,128)(2,1)}, bf16[1,3,128,384]{3,2,1,0:T(8,128)(2,1)S(1)}, u32[]{:S(2)}, u32[]{:S(2)}) collective-permute-start(bf16[1,3,128,384]{3,2,1,0:T(8,128)(2,1)} %get-tuple-element.43), channel_id=1, source_target_pairs={{1,0},{2,1},{3,2},{5,4},{6,5},{7,6},{9,8},{10,9},{11,10},{13,12},{... | collective-permute-start | bytes 884744 | tf_op jit(solution)/shard_map/ppermute | solution.py:189
  57.3 0.7 copy-start.9
  58.0 51.4 %collective-permute-start.14 = (bf16[1,4,128,384]{3,2,1,0:T(8,128)(2,1)}, bf16[1,4,128,384]{3,2,1,0:T(8,128)(2,1)S(1)}, u32[]{:S(2)}, u32[]{:S(2)}) collective-permute-start(bf16[1,4,128,384]{3,2,1,0:T(8,128)(2,1)} %get-tuple-element.47), channel_id=1, source_target_pairs={{0,1},{1,2},{2,3},{4,5},{5,6},{6,7},{8,9},{9,10},{10,11},{12,13},{... | collective-permute-start | bytes 1179656 | tf_op jit(solution)/shard_map/ppermute | solution.py:189
  61.1 0.8 copy-start.7
  61.8 47.5 %collective-permute-start.13 = (bf16[1,3,128,768]{3,2,1,0:T(8,128)(2,1)}, bf16[1,3,128,768]{3,2,1,0:T(8,128)(2,1)S(1)}, u32[]{:S(2)}, u32[]{:S(2)}) collective-permute-start(bf16[1,3,128,768]{3,2,1,0:T(8,128)(2,1)} %get-tuple-element.35), channel_id=1, source_target_pairs={{1,0},{2,1},{3,2},{5,4},{6,5},{7,6},{9,8},{10,9},{11,10},{13,12},{... | collective-permute-start | bytes 1769480 | tf_op jit(solution)/shard_map/ppermute | solution.py:189
  63.1 0.8 copy-start.3
  63.9 45.4 %collective-permute-start.12 = (bf16[1,4,128,768]{3,2,1,0:T(8,128)(2,1)}, bf16[1,4,128,768]{3,2,1,0:T(8,128)(2,1)S(1)}, u32[]{:S(2)}, u32[]{:S(2)}) collective-permute-start(bf16[1,4,128,768]{3,2,1,0:T(8,128)(2,1)} %get-tuple-element.39), channel_id=1, source_target_pairs={{0,1},{1,2},{2,3},{4,5},{5,6},{6,7},{8,9},{9,10},{10,11},{12,13},{... | collective-permute-start | bytes 2359304 | tf_op jit(solution)/shard_map/ppermute | solution.py:189
  68.8 1.1 copy-start.4
  69.8 1.0 copy-start.8
  70.8 1.0 copy-start.10
  71.8 37.6 %copy-start = (bf16[1,8,128,384]{3,2,1,0:T(8,128)(2,1)S(1)}, bf16[1,8,128,384]{3,2,1,0:T(8,128)(2,1)}, u32[]{:S(2)}) copy-start(bf16[1,8,128,384]{3,2,1,0:T(8,128)(2,1)} %get-tuple-element.45.refs_6_) | copy-start | bytes 2359300
  107.6 0.9 copy-start.1
  108.5 0.9 copy-start.5
  146.4 0.9 copy-start.2
  147.2 0.9 copy-start.6
  148.1 110.9 %reduce-scatter.7.cloned.1.call-start = ((), (), s32[]{:S(2)}) async-start(), calls=%async_computation.3 | async-start | bytes 1327104
  148.2 45.0 %collective-permute-start.8 = (bf16[1,1,128,768]{3,2,1,0:T(8,128)(2,1)S(1)}, bf16[1,1,128,768]{3,2,1,0:T(8,128)(2,1)}, u32[]{:S(2)}, u32[]{:S(2)}) collective-permute-start(bf16[1,1,128,768]{3,2,1,0:T(8,128)(2,1)S(1)} %get-tuple-element.15), channel_id=1, source_target_pairs={{1,0},{3,2},{5,4},{7,6},{9,8},{11,10},{13,12},{15,14},{17,16},{19,... | collective-permute-start | bytes 589832 | tf_op jit(solution)/shard_map/ppermute | solution.py:189
  149.5 67.9 %collective-permute-start.7 = (bf16[1,3,128,768]{3,2,1,0:T(8,128)(2,1)}, bf16[1,3,128,768]{3,2,1,0:T(8,128)(2,1)}, u32[]{:S(2)}, u32[]{:S(2)}) collective-permute-start(bf16[1,3,128,768]{3,2,1,0:T(8,128)(2,1)} %copy-done.5), channel_id=1, source_target_pairs={{0,1},{1,2},{2,3},{4,5},{5,6},{6,7},{8,9},{9,10},{10,11},{12,13},{... | collective-permute-start | bytes 1769480 | tf_op jit(solution)/shard_map/ppermute | solution.py:189
  154.6 62.8 %collective-permute-start.6 = (bf16[1,4,128,768]{3,2,1,0:T(8,128)(2,1)}, bf16[1,4,128,768]{3,2,1,0:T(8,128)(2,1)}, u32[]{:S(2)}, u32[]{:S(2)}) collective-permute-start(bf16[1,4,128,768]{3,2,1,0:T(8,128)(2,1)} %copy-done.1), channel_id=1, source_target_pairs={{1,0},{2,1},{3,2},{5,4},{6,5},{7,6},{9,8},{10,9},{11,10},{13,12},{... | collective-permute-start | bytes 2359304 | tf_op jit(solution)/shard_map/ppermute | solution.py:189
  155.9 39.6 %collective-permute-start.18 = (bf16[1,1,128,768]{3,2,1,0:T(8,128)(2,1)S(1)}, bf16[1,1,128,768]{3,2,1,0:T(8,128)(2,1)}, u32[]{:S(2)}, u32[]{:S(2)}) collective-permute-start(bf16[1,1,128,768]{3,2,1,0:T(8,128)(2,1)S(1)} %get-tuple-element.20), channel_id=1, source_target_pairs={{1,0},{3,2},{5,4},{7,6},{9,8},{11,10},{13,12},{15,14},{17,16},{19,... | collective-permute-start | bytes 589832 | tf_op jit(solution)/shard_map/ppermute | solution.py:189
  157.2 61.9 %collective-permute-start.17 = (bf16[1,3,128,768]{3,2,1,0:T(8,128)(2,1)}, bf16[1,3,128,768]{3,2,1,0:T(8,128)(2,1)}, u32[]{:S(2)}, u32[]{:S(2)}) collective-permute-start(bf16[1,3,128,768]{3,2,1,0:T(8,128)(2,1)} %copy-done.6), channel_id=1, source_target_pairs={{0,1},{1,2},{2,3},{4,5},{5,6},{6,7},{8,9},{9,10},{10,11},{12,13},{... | collective-permute-start | bytes 1769480 | tf_op jit(solution)/shard_map/ppermute | solution.py:189
  193.2 25.9 %collective-permute-start.16 = (bf16[1,4,128,768]{3,2,1,0:T(8,128)(2,1)}, bf16[1,4,128,768]{3,2,1,0:T(8,128)(2,1)S(1)}, u32[]{:S(2)}, u32[]{:S(2)}) collective-permute-start(bf16[1,4,128,768]{3,2,1,0:T(8,128)(2,1)} %copy-done.2), channel_id=1, source_target_pairs={{1,0},{2,1},{3,2},{5,4},{6,5},{7,6},{9,8},{10,9},{11,10},{13,12},{... | collective-permute-start | bytes 2359304 | tf_op jit(solution)/shard_map/ppermute | solution.py:189
  195.5 13.4 %collective-permute-start.9 = (bf16[1,1,128,768]{3,2,1,0:T(8,128)(2,1)S(1)}, bf16[1,1,128,768]{3,2,1,0:T(8,128)(2,1)S(1)}, u32[]{:S(2)}, u32[]{:S(2)}) collective-permute-start(bf16[1,1,128,768]{3,2,1,0:T(8,128)(2,1)S(1)} %fusion), channel_id=1, source_target_pairs={{2,0},{6,4},{10,8},{14,12},{18,16},{22,20},{26,24},{30,28}} | collective-permute-start | bytes 589832 | tf_op jit(solution)/shard_map/ppermute | solution.py:189
  208.9 7.6 %collective-permute-start.19 = (bf16[1,1,128,768]{3,2,1,0:T(8,128)(2,1)S(1)}, bf16[1,1,128,768]{3,2,1,0:T(8,128)(2,1)S(1)}, u32[]{:S(2)}, u32[]{:S(2)}) collective-permute-start(bf16[1,1,128,768]{3,2,1,0:T(8,128)(2,1)S(1)} %fusion.1), channel_id=1, source_target_pairs={{2,0},{6,4},{10,8},{14,12},{18,16},{22,20},{26,24},{30,28}} | collective-permute-start | bytes 589832 | tf_op jit(solution)/shard_map/ppermute | solution.py:189
Sparse Core Ops, SparseCore 0:
  148.3 42.2 reduce-scatter.4
  194.9 64.0 reduce-scatter.6

commit v2 on v0

--- a/solution.py
+++ b/solution.py
@@ -1,13 +1,520 @@
 import jax
 import jax.numpy as jnp
 from jax import lax
+from jax.experimental import pallas as pl
+from jax.experimental.pallas import tpu as pltpu
 from jax.sharding import PartitionSpec as P
 
 HD = 64
-
-
 SCALE = 0.125
 EPSILON = 1e-06
+LOW = 4
+HIGH = 3
+BAND = 8
+BANDS = 4
+SHARES = 8
+SLOTS = 1 + LOW + BAND + HIGH
+SUB = 8
+STEP = 16
+CELLS = SLOTS * SUB
+CHUNK = 64
+DEEP = 1024
+F32 = jnp.float32
+BF16 = jnp.bfloat16
+MESH = pl.DeviceIdType.MESH
+
+
+def dot(a, b, ca, cb):
+    return lax.dot_general(a, b, (((ca,), (cb,)), ((), ())), preferred_element_type=F32)
+
+
+def kernel(
+    code_in, x, g, w, out, wout,
+    code, hx, lx, ux, lg, ug, from_high, from_low, from_head,
+    normed_all, grads_all, mixed, acc, half_send, half_recv,
+    x_send, x_recv, y_send, y_recv, z_send, z_recv, fin, fin_recv,
+    code_ss, code_rs, halo_ss, halo_rs, head_ss, head_rs, back_ss, back_rs, top_ss, top_rs,
+    half_ss, half_rs, x_ss, x_rs, y_ss, y_rs, z_ss, z_rs, fin_ss, fin_rs,
+):
+    tables, _, cols, wide = x.shape
+    width = g.shape[-1]
+    per_table = cols // CHUNK
+    chunks = tables * per_table
+    band, share = lax.axis_index("band"), lax.axis_index("dp")
+    core, side = lax.rem(band, 2), band // 2
+    y, z = lax.rem(share, 2), share // 2
+    sibling, across = side * 2 + 1 - core, (1 - side) * 2 + core
+
+    def copy(src, dst, ss, rs, **where):
+        return pltpu.make_async_remote_copy(
+            src_ref=src, dst_ref=dst, send_sem=ss, recv_sem=rs, device_id=where, device_id_type=MESH
+        )
+
+    barrier = pltpu.get_barrier_semaphore()
+    for k in range(1, BANDS):
+        pl.semaphore_signal(
+            barrier, inc=1, device_id={"band": lax.rem(band + k, BANDS)}, device_id_type=MESH
+        )
+    pl.semaphore_signal(barrier, inc=1, device_id={"dp": z * 2 + 1 - y}, device_id_type=MESH)
+    for k in range(1, SHARES // 2):
+        other = lax.rem(z + k, SHARES // 2) * 2 + y
+        pl.semaphore_signal(barrier, inc=1, device_id={"dp": other}, device_id_type=MESH)
+    pl.semaphore_wait(barrier, BANDS + SHARES // 2 - 1)
+
+    def place(c):
+        return c // per_table, pl.ds(pl.multiple_of(lax.rem(c, per_table) * CHUNK, CHUNK), CHUNK)
+
+    def code_copy(k):
+        to = lax.rem(band + k, BANDS)
+        return copy(code_in.at[to], code.at[band], code_ss.at[k - 1], code_rs.at[k - 1], band=to)
+
+    def code_arrival(k):
+        source = lax.rem(band + BANDS - k, BANDS)
+        return copy(code_in.at[source], code.at[source], code_ss.at[k - 1], code_rs.at[k - 1], band=source)
+
+    def head_copy(c, to):
+        t, at = place(c)
+        return copy(
+            x.at[t, pl.ds(0, 1), at], hx.at[t, :, at], head_ss.at[to - 1, c], head_rs.at[c], band=to
+        )
+
+    def up_copies(c, to):
+        t, at = place(c)
+        rows = pl.ds(BAND - LOW, LOW)
+        return (
+            copy(x.at[t, rows, at], lx.at[t, :, at], halo_ss.at[0, c], halo_rs.at[0, c], band=to),
+            copy(g.at[t, rows, at], lg.at[t, :, at], halo_ss.at[1, c], halo_rs.at[1, c], band=to),
+        )
+
+    def down_copies(c, to):
+        t, at = place(c)
+        rows = pl.ds(0, HIGH)
+        return (
+            copy(x.at[t, rows, at], ux.at[t, :, at], halo_ss.at[2, c], halo_rs.at[2, c], band=to),
+            copy(g.at[t, rows, at], ug.at[t, :, at], halo_ss.at[3, c], halo_rs.at[3, c], band=to),
+        )
+
+    def back_low(c, to):
+        t, at = place(c)
+        return copy(lx.at[t, :, at], from_high.at[t, :, at], back_ss.at[0, c], back_rs.at[0, c], band=to)
+
+    def back_high(c, to):
+        t, at = place(c)
+        return copy(ux.at[t, :, at], from_low.at[t, :, at], back_ss.at[1, c], back_rs.at[1, c], band=to)
+
+    def back_head(c, source):
+        t, at = place(c)
+        return copy(
+            hx.at[t, :, at], from_head.at[source - 1, t, :, at], top_ss.at[c], top_rs.at[source - 1, c],
+            band=0,
+        )
+
+    has_low, has_high = band > 0, band < BANDS - 1
+
+    for k in range(1, BANDS):
+        code_copy(k).start()
+
+    def send_chunk(c, carry):
+        @pl.when(band == 0)
+        def _():
+            for to in range(1, BANDS):
+                head_copy(c, to).start()
+
+        @pl.when(has_high)
+        def _():
+            for one in up_copies(c, band + 1):
+                one.start()
+
+        @pl.when(has_low)
+        def _():
+            for one in down_copies(c, band - 1):
+                one.start()
+
+        return carry
+
+    lax.fori_loop(0, chunks, send_chunk, 0)
+
+    code[band] = code_in[band]
+
+    @pl.when(band == 0)
+    def _():
+        hx[...] = x[:, 0:1]
+        lx[...] = jnp.zeros_like(lx)
+        lg[...] = jnp.zeros_like(lg)
+
+    @pl.when(band == BANDS - 1)
+    def _():
+        ux[...] = jnp.zeros_like(ux)
+        ug[...] = jnp.zeros_like(ug)
+
+    for k in range(1, BANDS):
+        code_arrival(k).wait_recv()
+
+    lane = lax.broadcasted_iota(jnp.int32, (1, 128), 1)
+    left = jnp.where(lane < HD, 1.0, 0.0).astype(BF16)
+    right = jnp.where(lane < HD, 0.0, 1.0).astype(BF16)
+
+    def split_heads(a):
+        return jnp.concatenate((a * left, a * right), axis=0)
+
+    def flat(parts):
+        whole = jnp.concatenate(parts, axis=0).astype(F32)
+        return jnp.concatenate(
+            [whole[:, s : s + SUB].reshape(CELLS, whole.shape[-1]) for s in range(0, STEP, SUB)], axis=0
+        )
+
+    def step(t, at_step, many):
+        at = pl.ds(pl.multiple_of(at_step * STEP, STEP), STEP)
+        rows_all = pl.ds(pl.multiple_of(many * SLOTS * STEP, SLOTS * STEP), SLOTS * STEP)
+        states = flat((hx[t, :, at], lx[t, :, at], x[t, :, at], ux[t, :, at]))
+        inverse = lax.rsqrt(jnp.mean(states * states, axis=-1, keepdims=True) + EPSILON)
+        scaled = states * inverse
+        normed = scaled.astype(BF16)
+        normed_all[rows_all] = normed
+        mixed[...] = dot(normed, w[...], 1, 0).astype(BF16)
+        cotangent = flat((jnp.zeros((1, STEP, width), BF16), lg[t, :, at], g[t, :, at], ug[t, :, at]))
+        cotangent = cotangent.astype(BF16)
+        marks = code[at_step // 2, t, lax.rem(at_step, 2)]
+        biases = []
+        for s in range(STEP // SUB):
+            query_code = marks[s : s + 1]
+            key_code = jnp.broadcast_to(marks[s + 2 : s + 3], (CELLS, CELLS)).T
+            row = lax.broadcasted_iota(jnp.int32, (CELLS, CELLS), 0)
+            visible = (key_code == query_code) | (row == (query_code >> 3))
+            biases.append(jnp.where(visible, 0.0, -1e30).astype(F32))
+        units = [(s, p) for s in range(STEP // SUB) for p in range(width // 128)]
+
+        def part(kind, s, p):
+            start = kind * width + 128 * p
+            return mixed[s * CELLS : (s + 1) * CELLS, start : start + 128]
+
+        scale = jnp.asarray(SCALE, BF16)
+        grad = [cotangent[s * CELLS : (s + 1) * CELLS, 128 * p : 128 * p + 128] for s, p in units]
+        query = [part(0, s, p) * scale for s, p in units]
+        scores = [
+            dot(split_heads(part(1, s, p)), q, 1, 1).reshape(2, CELLS, CELLS)
+            for (s, p), q in zip(units, query)
+        ]
+        prob_grad = [
+            dot(split_heads(part(2, s, p)), d, 1, 1).reshape(2, CELLS, CELLS)
+            for (s, p), d in zip(units, grad)
+        ]
+        all_grads = {}
+        for n, (s, p) in enumerate(units):
+            masked = scores[n] + biases[s][None]
+            peak = jnp.maximum(jnp.max(masked, axis=1, keepdims=True), -1e29)
+            expsc = jnp.exp(masked - peak)
+            total = jnp.maximum(jnp.sum(expsc, axis=1, keepdims=True), 1.0)
+            probs = expsc * (1.0 / total)
+            delta = jnp.sum(probs * prob_grad[n], axis=1, keepdims=True)
+            score_low = (probs * (prob_grad[n] - delta)).astype(BF16)
+            probs_low = probs.astype(BF16)
+            value_grad = dot(
+                jnp.concatenate((probs_low[0], probs_low[1]), axis=1), split_heads(grad[n]), 1, 0
+            )
+            key_grad = dot(
+                jnp.concatenate((score_low[0], score_low[1]), axis=1), split_heads(query[n]), 1, 0
+            )
+            query_grad = dot(
+                score_low.reshape(2 * CELLS, CELLS), split_heads(part(1, s, p) * scale), 0, 0
+            )
+            all_grads[s, 0, p] = query_grad.astype(BF16)
+            all_grads[s, 1, p] = key_grad.astype(BF16)
+            all_grads[s, 2, p] = value_grad.astype(BF16)
+        joined = jnp.concatenate(
+            [
+                jnp.concatenate([all_grads[s, k, p] for k in range(3) for p in range(width // 128)], axis=1)
+                for s in range(STEP // SUB)
+            ],
+            axis=0,
+        )
+        grads_all[rows_all] = joined
+        normed_grad = dot(joined, w[...], 1, 1)
+        coupling = jnp.mean(normed_grad * scaled, axis=-1, keepdims=True)
+        result = inverse * (normed_grad - scaled * coupling)
+        pieces = [result[s * CELLS : (s + 1) * CELLS].reshape(SLOTS, SUB, wide) for s in range(STEP // SUB)]
+        result = jnp.concatenate(pieces, axis=1).astype(BF16)
+        hx[t, :, at] = result[:1]
+        lx[t, :, at] = result[1 : 1 + LOW]
+        out[t, :, at] = result[1 + LOW : 1 + LOW + BAND]
+        ux[t, :, at] = result[1 + LOW + BAND :]
+
+    steps = CHUNK // STEP
+
+    def work_chunk(c, carry):
+        @pl.when(band > 0)
+        def _():
+            head_copy(c, 1).wait_recv()
+
+        @pl.when(has_low)
+        def _():
+            for one in up_copies(c, 0):
+                one.wait_recv()
+
+        @pl.when(has_high)
+        def _():
+            for one in down_copies(c, 0):
+                one.wait_recv()
+
+        def one_step(i, carry):
+            step(c // per_table, lax.rem(c, per_table) * steps + i, c * steps + i)
+            return carry
+
+        lax.fori_loop(0, steps, one_step, 0)
+
+        @pl.when(has_low)
+        def _():
+            back_low(c, band - 1).start()
+
+        @pl.when(has_high)
+        def _():
+            back_high(c, band + 1).start()
+
+        for source in range(1, BANDS):
+
+            @pl.when(band == source)
+            def _():
+                back_head(c, source).start()
+
+        return carry
+
+    lax.fori_loop(0, chunks, work_chunk, 0)
+
+    total_rows = grads_all.shape[0]
+    block = 3 * width // SHARES
+    rows_half = SHARES // 2 * block
+    mine = pl.ds(pl.multiple_of(core * rows_half, 16), rows_half)
+    theirs = pl.ds(pl.multiple_of((1 - core) * rows_half, 16), rows_half)
+
+    def product(n, which):
+        lanes = pl.ds(pl.multiple_of(which * (wide // 2), 128), wide // 2)
+        acc[n] = jnp.zeros(acc.shape[1:], F32)
+
+        def deep(i, carry):
+            at = pl.ds(pl.multiple_of(i * DEEP, DEEP), DEEP)
+            acc[n] += dot(grads_all[at, :], normed_all[at, lanes], 0, 0)
+            return carry
+
+        lax.fori_loop(0, total_rows // DEEP, deep, 0)
+        half_send[n] = acc[n, theirs, :].astype(BF16)
+
+    def half_copy(n):
+        return copy(half_send.at[n], half_recv.at[n], half_ss.at[n], half_rs.at[n], band=sibling)
+
+    product(0, 1 - side)
+    half_copy(0).start()
+    product(1, side)
+    half_copy(1).start()
+    half_copy(0).wait_recv()
+    x_send[...] = (acc[0, mine, :] + half_recv[0].astype(F32)).astype(BF16)
+    x_copy = copy(x_send, x_recv, x_ss, x_rs, band=across)
+    x_copy.start()
+
+    def merge_chunk(c, carry):
+        t, at = place(c)
+
+        @pl.when(has_high)
+        def _():
+            back_low(c, 0).wait_recv()
+            rows = pl.ds(BAND - LOW, LOW)
+            out[t, rows, at] = (out[t, rows, at].astype(F32) + from_high[t, :, at].astype(F32)).astype(BF16)
+
+        @pl.when(has_low)
+        def _():
+            back_high(c, 0).wait_recv()
+            rows = pl.ds(0, HIGH)
+            out[t, rows, at] = (out[t, rows, at].astype(F32) + from_low[t, :, at].astype(F32)).astype(BF16)
+
+        @pl.when(band == 0)
+        def _():
+            top = out[t, 0:1, at].astype(F32) + hx[t, :, at].astype(F32)
+            for source in range(1, BANDS):
+                back_head(c, source).wait_recv()
+                top = top + from_head[source - 1, t, :, at].astype(F32)
+            out[t, 0:1, at] = top.astype(BF16)
+
+        return carry
+
+    lax.fori_loop(0, chunks, merge_chunk, 0)
+
+    half_copy(1).wait_recv()
+    x_copy.wait_recv()
+    kept = acc[1, mine, :] + half_recv[1].astype(F32) + x_recv[...].astype(F32)
+    kept = kept.reshape(SHARES // 4, 2, block, wide // 2)
+    acc_y = jnp.where(y == 0, kept[:, 0], kept[:, 1])
+    y_send[...] = jnp.where(y == 0, kept[:, 1], kept[:, 0]).astype(BF16)
+    y_copy = copy(y_send, y_recv, y_ss, y_rs, dp=z * 2 + 1 - y)
+    y_copy.start()
+    y_copy.wait_recv()
+    acc_z = acc_y + y_recv[...].astype(F32)
+    z_send[...] = acc_z.astype(BF16)
+
+    def z_copy(j, source):
+        return copy(z_send.at[j], z_recv.at[source], z_ss.at[j], z_rs.at[source], dp=(2 * core + j) * 2 + y)
+
+    zs = SHARES // 2
+    for j in range(2):
+        for source in range(zs):
+
+            @pl.when((z == source) & (2 * core + j != z))
+            def _():
+                z_copy(j, source).start()
+
+    fin_copy = copy(fin, fin_recv, fin_ss, fin_rs, band=sibling)
+    holder = z // 2 == core
+
+    def emit(full):
+        half = wide // 4
+        wout[...] = jnp.where(core == 0, full[:, :half], full[:, half:])
+
+    @pl.when(holder)
+    def _():
+        fin[...] = jnp.where(lax.rem(z, 2) == 0, acc_z[0], acc_z[1])
+        for source in range(zs):
+
+            @pl.when(z != source)
+            def _():
+                z_copy(0, source).wait_recv()
+                fin[...] += z_recv[source].astype(F32)
+
+        fin_copy.start()
+        emit(fin[...])
+        fin_copy.wait_send()
+
+    @pl.when(jnp.logical_not(holder))
+    def _():
+        fin_copy.wait_recv()
+        emit(fin_recv[...])
+
+    for k in range(1, BANDS):
+        code_copy(k).wait_send()
+
+    def drain(c, carry):
+        @pl.when(band == 0)
+        def _():
+            for to in range(1, BANDS):
+                head_copy(c, to).wait_send()
+
+        @pl.when(has_high)
+        def _():
+            for one in up_copies(c, band + 1):
+                one.wait_send()
+            back_high(c, band + 1).wait_send()
+
+        @pl.when(has_low)
+        def _():
+            for one in down_copies(c, band - 1):
+                one.wait_send()
+            back_low(c, band - 1).wait_send()
+            back_head(c, 1).wait_send()
+
+        return carry
+
+    lax.fori_loop(0, chunks, drain, 0)
+    half_copy(0).wait_send()
+    half_copy(1).wait_send()
+    x_copy.wait_send()
+    y_copy.wait_send()
+    for j in range(2):
+
+        @pl.when(2 * core + j != z)
+        def _():
+            z_copy(j, 0).wait_send()
+
+
+def group_codes(group_ids):
+    rows = group_ids.shape[-1]
+    same = group_ids[:, :, :, None] == group_ids[:, :, None, :]
+    at = jnp.arange(rows)
+    before = jnp.sum(same & (at[None, :] < at[:, None]), axis=-1)
+    after = jnp.sum(same & (at[None, :] > at[:, None]), axis=-1)
+    start, end = at - before, at + after
+    first, last = start // BAND, end // BAND
+    border = last * BAND
+    owner = jnp.where((first != last) & (border - start > end + 1 - border), first, last)
+    return (group_ids + 8 * owner).astype(jnp.int32)
+
+
+def slot_codes(codes, band):
+    tables, cols, rows = codes.shape
+    padded = jnp.pad(codes, ((0, 0), (0, 0), (LOW, HIGH)), constant_values=-8)
+    near = padded[:, :, band * BAND : band * BAND + LOW + BAND + HIGH]
+    row = band * BAND - LOW + jnp.arange(LOW + BAND + HIGH)
+    alive = (near >> 3) == band
+    mark = (jnp.arange(cols) % SUB)[None, :, None] * 8 + (near & 7)
+    query = jnp.where(alive, mark, -1)
+    key = jnp.where(alive & (row != 0), mark, -2)
+
+    def order(values, header):
+        values = jnp.pad(values, ((0, 0), (0, 0), (1, 0)), constant_values=header)
+        values = values.reshape(tables, cols // STEP, STEP // SUB, SUB, SLOTS)
+        return values.transpose(0, 1, 2, 4, 3).reshape(tables, cols // STEP, STEP // SUB, CELLS)
+
+    return jnp.concatenate((order(query, -1), order(key, -2)), axis=2).astype(jnp.int32)
+
+
+def halo_body(cell_states, head_grads, group_ids, proj_weights):
+    tables, _, cols, wide = cell_states.shape
+    width = head_grads.shape[-1]
+    codes = group_codes(group_ids)
+    codes = jnp.stack([slot_codes(codes, b) for b in range(BANDS)])
+    chunks = tables * cols // CHUNK
+    many = SLOTS * tables * cols
+    block = 3 * width // SHARES
+    rows_half, lanes = 3 * width // 2, wide // 2
+    halo = lambda rows, features: pltpu.VMEM((tables, rows, cols, features), BF16)
+    sems = lambda *shape: pltpu.SemaphoreType.DMA(shape)
+    pair = lambda *shape: [sems(*shape), sems(*shape)]
+    one = pltpu.SemaphoreType.DMA
+    vmem = pl.BlockSpec(memory_space=pltpu.VMEM)
+    input_grad, turned = pl.pallas_call(
+        kernel,
+        in_specs=[vmem] * 4,
+        out_specs=[vmem] * 2,
+        out_shape=[
+            jax.ShapeDtypeStruct(cell_states.shape, BF16),
+            jax.ShapeDtypeStruct((block, wide // BANDS), F32),
+        ],
+        scratch_shapes=[
+            pltpu.VMEM(codes.shape, jnp.int32),
+            halo(1, wide), halo(LOW, wide), halo(HIGH, wide), halo(LOW, width), halo(HIGH, width),
+            halo(LOW, wide), halo(HIGH, wide),
+            pltpu.VMEM((BANDS - 1, tables, 1, cols, wide), BF16),
+            pltpu.VMEM((many, wide), BF16),
+            pltpu.VMEM((many, 3 * width), BF16),
+            pltpu.VMEM((SLOTS * STEP, 3 * width), BF16),
+            pltpu.VMEM((2, 3 * width, lanes), F32),
+            pltpu.VMEM((2, rows_half, lanes), BF16),
+            pltpu.VMEM((2, rows_half, lanes), BF16),
+            pltpu.VMEM((rows_half, lanes), BF16),
+            pltpu.VMEM((rows_half, lanes), BF16),
+            pltpu.VMEM((2, block, lanes), BF16),
+            pltpu.VMEM((2, block, lanes), BF16),
+            pltpu.VMEM((2, block, lanes), BF16),
+            pltpu.VMEM((SHARES // 2, block, lanes), BF16),
+            pltpu.VMEM((block, lanes), F32),
+            pltpu.VMEM((block, lanes), F32),
+            *pair(BANDS - 1),
+            *pair(4, chunks),
+            sems(BANDS - 1, chunks), sems(chunks),
+            *pair(2, chunks),
+            sems(chunks), sems(BANDS - 1, chunks),
+            *pair(2),
+            one, one,
+            one, one,
+            sems(2), sems(SHARES // 2),
+            one, one,
+        ],
+        compiler_params=pltpu.CompilerParams(
+            collective_id=0, has_side_effects=True, vmem_limit_bytes=60 * 1024 * 1024
+        ),
+        cost_estimate=pl.CostEstimate(
+            flops=6 * many * wide * 3 * width + 10 * many * 128 * width * 2,
+            bytes_accessed=many * (2 * wide + width),
+            transcendentals=many * 128 * 6,
+        ),
+    )(codes, cell_states, head_grads, proj_weights)
+    return (input_grad, turned.T)
 
 
 def normalize(states):
@@ -76,7 +583,7 @@
     return (partial_w, state_grad)
 
 
-def body(cell_states, head_grads, group_ids, proj_weights):
+def exchange_body(cell_states, head_grads, group_ids, proj_weights):
     scaled, inverse, normed = normalize(cell_states)
     query_rows, key_rows, value_rows = project(normed, proj_weights)
     query_cols, key_cols, value_cols, grad_cols = (
@@ -98,6 +605,13 @@
     shared = lax.psum_scatter(partial_w, "dp", scatter_dimension=1, tiled=True)
     weight_grad = lax.psum_scatter(shared, "band", scatter_dimension=0, tiled=True)
     return (input_grad, weight_grad)
+
+
+def body(cell_states, head_grads, group_ids, proj_weights):
+    halo = cell_states.shape[1] == BAND
+    halo = halo and lax.axis_size("band") == BANDS and lax.axis_size("dp") == SHARES
+    form = halo_body if halo else exchange_body
+    return form(cell_states, head_grads, group_ids, proj_weights)
 
 
 def solution(mesh):

time: 380 us -> 109 us (0.29); the launches traced: 373 us -> 108 us
  waiting for transfers between devices: 164 us -> 0 us
  Pallas kernels: 0 us -> 95.2 us
  local copies, waits for them, and re-layouts: 82.9 us -> 6.62 us
  matrix products: 69.3 us -> 0 us
  starting transfers between devices: 30.2 us -> 0 us
  between operations: 14.5 us -> 0.76 us
  other arithmetic: 11.5 us -> 5.22 us
    pallas_call x0 -> x1, Pallas kernels: none -> 95.2 us  [halo_body(): pl.pallas_call(kernel, in_specs=[vmem] * 4, out_specs=[vmem] * 2, out_sha...]
    reduce_scatter x1 -> x0, waiting for transfers between devices: 80.2 us -> none  [body(): shared = lax.psum_scatter(partial_w, 'dp', scatter_dimension=1, tiled=True)]
    all_to_all x7 -> x0, waiting for transfers between devices: 70.5 us -> none  [the longest x1 16.7 us: body(): lax.all_to_all(value_rows, 'band', split_axis=2, concat_axis=1, tiled=True)]
    dot_general x8 -> x0, matrix products: 69.3 us -> none  [the longest x1 15.1 us: attend_back(): jnp.einsum('bchij,bichd->bjchd', score_low, query_five, preferred_element...]
    reshape x10 -> x16, local copies, waits for them, and re-layouts: 49.1 us -> 1.47 us  [the longest x8 0.87 us: order(): values.transpose(0, 1, 2, 4, 3)]
    all_to_all x7 -> x0, starting transfers between devices: 29.9 us -> none  [the longest x1 4.6 us: body(): lax.all_to_all(head_grads, 'band', split_axis=2, concat_axis=1, tiled=True)]
    unnamed x28 -> x4, local copies, waits for them, and re-layouts: 18.8 us -> 4.53 us
    unnamed x3 -> x0, waiting for transfers between devices: 13.6 us -> none
  transfers between devices with their start and end apart: 9 -> 0, of which waited for: 8 -> 0; matrix products, arithmetic and copies ran while one was open for 23% -> 0% of each run, Pallas kernels for 0% -> 0%
where the time goes in v2:
time: 109 us; the launch traced here: 108 us
  Pallas kernels  95.2 us (87%)
  local copies, waits for them, and re-layouts  6.62 us (6%)
  other arithmetic  5.22 us (5%)
    pallas_call x1, Pallas kernels, halo_body(): pl.pallas_call(kernel, in_specs=[vmem] * 4, out_specs=[vmem] * 2, out_sha...  95.2 us
    unnamed x4, local copies, waits for them, and re-layouts  4.53 us
    reduce_sum x1, other arithmetic, group_codes(): after = jnp.sum(same & (at[None, :] > at[:, None]), axis=-1)  3.48 us

profile of v2, /device:TPU:0, one launch (start us, length us, event | category | flops | bytes accessed | tf_op | source)
XLA Modules:
  0.0 107.8 jit_solution(4588922758839346866)
XLA Ops:
  0.7 3.5 %convert_reduce_fusion = (s32[2,32,32]{2,1,0:T(8,128)S(1)}, s32[2,32,32]{2,1,0:T(8,128)S(1)}) fusion(s32[2,32,32]{2,1,0:T(8,128)} %param.6, pred[32,32]{1,0:T(8,128)(4,1)S(1)} %get-tuple-element.26, pred[32,32]{1,0:T(8,128)(4,1)S(1)} %get-tuple-element.27), kind=kLoop, calls=%fused_computation.2 | loop fusion | flops 454656 | bytes 26624 | tf_op jit(solution)/shard_map/reduce_sum | solution.py:430
  4.2 0.8 multiply_add_fusion
  5.0 0.1 fusion.5
  5.1 0.1 pad.33
  5.2 0.1 copy.22
  5.3 0.1 reshape.110
  5.4 0.1 pad.35
  5.5 0.1 copy.24
  5.5 0.1 reshape.114
  5.7 0.1 pad.37
  5.7 0.1 pad.39
  5.8 0.1 copy.26
  5.9 0.1 reshape.118
  6.0 0.1 copy.28
  6.1 0.1 reshape.122
  6.2 0.1 and_select_fusion.3
  6.3 0.1 pad.34
  6.4 0.1 copy.23
  6.5 0.1 reshape.112
  6.6 0.1 pad.40
  6.7 0.1 copy.29
  6.7 0.1 reshape.124
  6.9 0.1 pad.38
  6.9 0.1 pad.36
  7.0 0.1 copy.27
  7.1 0.1 reshape.120
  7.2 0.1 copy.25
  7.3 0.1 reshape.116
  7.4 0.6 pad_add_fusion.code_in
  8.0 95.2 %shard_map.59 = (bf16[2,8,128,768]{3,2,1,0:T(8,128)(2,1)}, f32[144,192]{1,0:T(8,128)}) custom-call(s32[4,2,2,4,128]{4,3,2,1,0:T(4,128)} %pad_add_fusion.code_in, bf16[2,8,128,768]{3,2,1,0:T(8,128)(2,1)} %x.19, bf16[2,8,128,384]{3,2,1,0:T(8,128)(2,1)} %g.1, bf16[768,1152]{1,0:T(8,128)(2,1)} %w.1), custom_call_target="tpu_custom_call" | custom-call | flops 25769803776 | bytes 7864320 | tf_op jit(solution)/shard_map/pallas_call | solution.py:470
  103.3 0.0 copy-start
  103.3 3.9 %copy.32 = bf16[2,8,128,768]{3,2,1,0:T(8,128)(2,1)} copy(bf16[2,8,128,768]{3,2,1,0:T(8,128)(2,1)} %get-tuple-element.34) | data formatting | bytes 6291456
  107.2 0.0 copy-done
  107.2 0.7 copy.33
  (8 shorter events, 0.1 us)
Async XLA Ops:
  103.3 3.9 %copy-start = (f32[144,192]{1,0:T(8,128)S(1)}, f32[144,192]{1,0:T(8,128)}, u32[]{:S(2)}) copy-start(f32[144,192]{1,0:T(8,128)} %get-tuple-element.5) | copy-start | bytes 331780

commit v3 on v2

--- a/solution.py
+++ b/solution.py
@@ -15,9 +15,10 @@
 SHARES = 8
 SLOTS = 1 + LOW + BAND + HIGH
 SUB = 8
-STEP = 16
+STEP = 32
 CELLS = SLOTS * SUB
-CHUNK = 64
+CHUNK = 32
+AHEAD = 2
 DEEP = 1024
 F32 = jnp.float32
 BF16 = jnp.bfloat16
@@ -40,6 +41,7 @@
     width = g.shape[-1]
     per_table = cols // CHUNK
     chunks = tables * per_table
+    per_band = cols // BANDS // STEP
     band, share = lax.axis_index("band"), lax.axis_index("dp")
     core, side = lax.rem(band, 2), band // 2
     y, z = lax.rem(share, 2), share // 2
@@ -132,7 +134,7 @@
 
         return carry
 
-    lax.fori_loop(0, chunks, send_chunk, 0)
+    lax.fori_loop(0, AHEAD, send_chunk, 0)
 
     code[band] = code_in[band]
 
@@ -174,11 +176,11 @@
         mixed[...] = dot(normed, w[...], 1, 0).astype(BF16)
         cotangent = flat((jnp.zeros((1, STEP, width), BF16), lg[t, :, at], g[t, :, at], ug[t, :, at]))
         cotangent = cotangent.astype(BF16)
-        marks = code[at_step // 2, t, lax.rem(at_step, 2)]
+        marks = code[at_step // per_band, t, lax.rem(at_step, per_band)]
         biases = []
         for s in range(STEP // SUB):
             query_code = marks[s : s + 1]
-            key_code = jnp.broadcast_to(marks[s + 2 : s + 3], (CELLS, CELLS)).T
+            key_code = jnp.broadcast_to(marks[STEP // SUB + s : STEP // SUB + s + 1], (CELLS, CELLS)).T
             row = lax.broadcasted_iota(jnp.int32, (CELLS, CELLS), 0)
             visible = (key_code == query_code) | (row == (query_code >> 3))
             biases.append(jnp.where(visible, 0.0, -1e30).astype(F32))
@@ -256,6 +258,10 @@
             for one in down_copies(c, 0):
                 one.wait_recv()
 
+        @pl.when(c + AHEAD < chunks)
+        def _():
+            send_chunk(c + AHEAD, 0)
+
         def one_step(i, carry):
             step(c // per_table, lax.rem(c, per_table) * steps + i, c * steps + i)
             return carry
@@ -286,29 +292,39 @@
     mine = pl.ds(pl.multiple_of(core * rows_half, 16), rows_half)
     theirs = pl.ds(pl.multiple_of((1 - core) * rows_half, 16), rows_half)
 
-    def product(n, which):
+    def product(n, which, begin, end):
         lanes = pl.ds(pl.multiple_of(which * (wide // 2), 128), wide // 2)
-        acc[n] = jnp.zeros(acc.shape[1:], F32)
 
         def deep(i, carry):
             at = pl.ds(pl.multiple_of(i * DEEP, DEEP), DEEP)
             acc[n] += dot(grads_all[at, :], normed_all[at, lanes], 0, 0)
             return carry
 
-        lax.fori_loop(0, total_rows // DEEP, deep, 0)
-        half_send[n] = acc[n, theirs, :].astype(BF16)
+        lax.fori_loop(begin, end, deep, 0)
 
     def half_copy(n):
         return copy(half_send.at[n], half_recv.at[n], half_ss.at[n], half_rs.at[n], band=sibling)
 
-    product(0, 1 - side)
+    def x_copy(j):
+        return copy(x_send.at[j], x_recv.at[j], x_ss.at[j], x_rs.at[j], band=across)
+
+    def piece(j):
+        return pl.ds(pl.multiple_of(core * rows_half + j * (2 * block), 16), 2 * block)
+
+    deeps = total_rows // DEEP
+    acc[...] = jnp.zeros_like(acc)
+    product(0, 1 - side, 0, deeps)
+    half_send[0] = acc[0, theirs, :].astype(BF16)
     half_copy(0).start()
-    product(1, side)
+    product(1, side, 0, 1)
+    half_copy(0).wait_recv()
+    for j in range(2):
+        partner = half_recv[0, 2 * block * j : 2 * block * (j + 1)].astype(F32)
+        x_send[j] = (acc[0, piece(j), :] + partner).astype(BF16)
+        x_copy(j).start()
+    product(1, side, 1, deeps)
+    half_send[1] = acc[1, theirs, :].astype(BF16)
     half_copy(1).start()
-    half_copy(0).wait_recv()
-    x_send[...] = (acc[0, mine, :] + half_recv[0].astype(F32)).astype(BF16)
-    x_copy = copy(x_send, x_recv, x_ss, x_rs, band=across)
-    x_copy.start()
 
     def merge_chunk(c, carry):
         t, at = place(c)
@@ -337,23 +353,28 @@
 
     lax.fori_loop(0, chunks, merge_chunk, 0)
 
+    def y_copy(j):
+        return copy(y_send.at[j], y_recv.at[j], y_ss.at[j], y_rs.at[j], dp=z * 2 + 1 - y)
+
     half_copy(1).wait_recv()
-    x_copy.wait_recv()
-    kept = acc[1, mine, :] + half_recv[1].astype(F32) + x_recv[...].astype(F32)
-    kept = kept.reshape(SHARES // 4, 2, block, wide // 2)
-    acc_y = jnp.where(y == 0, kept[:, 0], kept[:, 1])
-    y_send[...] = jnp.where(y == 0, kept[:, 1], kept[:, 0]).astype(BF16)
-    y_copy = copy(y_send, y_recv, y_ss, y_rs, dp=z * 2 + 1 - y)
-    y_copy.start()
-    y_copy.wait_recv()
-    acc_z = acc_y + y_recv[...].astype(F32)
-    z_send[...] = acc_z.astype(BF16)
+    kept_y = []
+    for j in range(2):
+        x_copy(j).wait_recv()
+        kept = acc[1, piece(j), :] + half_recv[1, 2 * block * j : 2 * block * (j + 1)].astype(F32)
+        kept = (kept + x_recv[j].astype(F32)).reshape(2, block, wide // 2)
+        kept_y.append(jnp.where(y == 0, kept[0], kept[1]))
+        y_send[j] = jnp.where(y == 0, kept[1], kept[0]).astype(BF16)
+        y_copy(j).start()
 
     def z_copy(j, source):
         return copy(z_send.at[j], z_recv.at[source], z_ss.at[j], z_rs.at[source], dp=(2 * core + j) * 2 + y)
 
     zs = SHARES // 2
+    acc_z = []
     for j in range(2):
+        y_copy(j).wait_recv()
+        acc_z.append(kept_y[j] + y_recv[j].astype(F32))
+        z_send[j] = acc_z[j].astype(BF16)
         for source in range(zs):
 
             @pl.when((z == source) & (2 * core + j != z))
@@ -413,9 +434,9 @@
     lax.fori_loop(0, chunks, drain, 0)
     half_copy(0).wait_send()
     half_copy(1).wait_send()
-    x_copy.wait_send()
-    y_copy.wait_send()
     for j in range(2):
+        x_copy(j).wait_send()
+        y_copy(j).wait_send()
 
         @pl.when(2 * core + j != z)
         def _():
@@ -423,16 +444,19 @@
 
 
 def group_codes(group_ids):
-    rows = group_ids.shape[-1]
-    same = group_ids[:, :, :, None] == group_ids[:, :, None, :]
-    at = jnp.arange(rows)
-    before = jnp.sum(same & (at[None, :] < at[:, None]), axis=-1)
-    after = jnp.sum(same & (at[None, :] > at[:, None]), axis=-1)
-    start, end = at - before, at + after
-    first, last = start // BAND, end // BAND
-    border = last * BAND
-    owner = jnp.where((first != last) & (border - start > end + 1 - border), first, last)
-    return (group_ids + 8 * owner).astype(jnp.int32)
+    bands = group_ids.reshape(group_ids.shape[:2] + (BANDS, BAND))
+    first = bands[..., :1]
+    following = jnp.pad(first[:, :, 1:], ((0, 0), (0, 0), (0, 1), (0, 0)), constant_values=-1)
+    tail = bands == following
+    head = bands == first
+    below = jnp.sum(tail, axis=-1, keepdims=True)
+    above = jnp.sum(head, axis=-1, keepdims=True)
+    above_next = jnp.pad(above[:, :, 1:], ((0, 0), (0, 0), (0, 1), (0, 0)))
+    below_last = jnp.pad(below[:, :, :-1], ((0, 0), (0, 0), (1, 0), (0, 0)))
+    goes_up = tail & (below <= above_next)
+    goes_down = head & (below_last > above)
+    owner = jnp.arange(BANDS)[:, None] + goes_up.astype(jnp.int32) - goes_down.astype(jnp.int32)
+    return (bands + 8 * owner).astype(jnp.int32).reshape(group_ids.shape)
 
 
 def slot_codes(codes, band):
@@ -486,8 +510,8 @@
             pltpu.VMEM((2, 3 * width, lanes), F32),
             pltpu.VMEM((2, rows_half, lanes), BF16),
             pltpu.VMEM((2, rows_half, lanes), BF16),
-            pltpu.VMEM((rows_half, lanes), BF16),
-            pltpu.VMEM((rows_half, lanes), BF16),
+            pltpu.VMEM((2, 2 * block, lanes), BF16),
+            pltpu.VMEM((2, 2 * block, lanes), BF16),
             pltpu.VMEM((2, block, lanes), BF16),
             pltpu.VMEM((2, block, lanes), BF16),
             pltpu.VMEM((2, block, lanes), BF16),
@@ -500,8 +524,8 @@
             *pair(2, chunks),
             sems(chunks), sems(BANDS - 1, chunks),
             *pair(2),
-            one, one,
-            one, one,
+            *pair(2),
+            *pair(2),
             sems(2), sems(SHARES // 2),
             one, one,
         ],

time: 109 us -> 97.6 us (0.90)
  the two profiles are of different devices: /device:TPU:0 before, /device:TPU:9 now
where the time goes in v3:
time: 97.6 us; the launch traced here: 97.4 us
  Pallas kernels  87.5 us (90%)
  local copies, waits for them, and re-layouts  8.31 us (9%)
    pallas_call x1, Pallas kernels, halo_body(): pl.pallas_call(kernel, in_specs=[vmem] * 4, out_specs=[vmem] * 2, out_sha...  87.5 us
    unnamed x13, local copies, waits for them, and re-layouts  6.1 us

profile of v3, /device:TPU:9, one launch (start us, length us, event | category | flops | bytes accessed | tf_op | source)
XLA Modules:
  0.0 97.4 jit_solution(18380984930222319650)
XLA Ops:
  0.7 0.1 add.124
  0.8 0.8 copy.29
  1.7 0.1 multiply_add_fusion
  1.8 0.1 copy.46
  1.9 0.1 pad_bitcast_fusion.7
  2.0 0.1 and_select_fusion.3
  2.1 0.1 copy.47
  2.2 0.1 pad_bitcast_fusion.6
  2.2 0.1 copy.33
  2.3 0.1 reshape.96
  2.4 0.1 copy.51
  2.5 0.1 pad_bitcast_fusion.2
  2.6 0.1 copy.41
  2.7 0.1 reshape.104
  2.8 0.1 copy.49
  2.9 0.1 pad_bitcast_fusion.4
  2.9 0.1 copy.37
  3.0 0.1 reshape.100
  3.1 0.1 copy.53
  3.2 0.1 pad_bitcast_fusion
  3.3 0.1 copy.45
  3.4 0.1 reshape.108
  3.5 0.1 copy.31
  3.6 0.1 reshape.94
  3.7 0.1 copy.48
  3.8 0.1 pad_bitcast_fusion.5
  3.9 0.1 copy.35
  3.9 0.1 reshape.98
  4.1 0.1 copy.50
  4.2 0.1 pad_bitcast_fusion.3
  4.2 0.1 copy.39
  4.3 0.1 reshape.102
  4.4 0.1 copy.52
  4.5 0.1 pad_bitcast_fusion.1
  4.6 0.1 copy.43
  4.7 0.1 reshape.106
  4.8 0.6 pad_add_fusion.code_in
  5.4 87.5 %shard_map.59 = (bf16[2,8,128,768]{3,2,1,0:T(8,128)(2,1)}, f32[144,192]{1,0:T(8,128)}) custom-call(s32[4,2,1,8,128]{4,3,2,1,0:T(8,128)} %pad_add_fusion.code_in, bf16[2,8,128,768]{3,2,1,0:T(8,128)(2,1)} %x.25, bf16[2,8,128,384]{3,2,1,0:T(8,128)(2,1)} %g.1, bf16[768,1152]{1,0:T(8,128)(2,1)} %w.1), custom_call_target="tpu_custom_call" | custom-call | flops 25769803776 | bytes 7864320 | tf_op jit(solution)/shard_map/pallas_call | solution.py:494
  92.9 0.0 copy-start
  92.9 3.9 %copy.56 = bf16[2,8,128,768]{3,2,1,0:T(8,128)(2,1)} copy(bf16[2,8,128,768]{3,2,1,0:T(8,128)(2,1)} %get-tuple-element.34) | data formatting | bytes 6291456
  96.8 0.0 copy-done
  96.8 0.7 copy.57
  (15 shorter events, 0.2 us)
Async XLA Ops:
  92.9 3.9 %copy-start = (f32[144,192]{1,0:T(8,128)S(1)}, f32[144,192]{1,0:T(8,128)}, u32[]{:S(2)}) copy-start(f32[144,192]{1,0:T(8,128)} %get-tuple-element.5) | copy-start | bytes 331780

commit v4 on v3

--- a/solution.py
+++ b/solution.py
@@ -17,8 +17,9 @@
 SUB = 8
 STEP = 32
 CELLS = SLOTS * SUB
-CHUNK = 32
+CHUNK = STEP
 AHEAD = 2
+LATE = 4
 DEEP = 1024
 F32 = jnp.float32
 BF16 = jnp.bfloat16
@@ -30,15 +31,16 @@
 
 
 def kernel(
-    code_in, x, g, w, out, wout,
+    code_in, x_in, g_in, w_in, out, wout, x, g, w,
     code, hx, lx, ux, lg, ug, from_high, from_low, from_head,
-    normed_all, grads_all, mixed, acc, half_send, half_recv,
-    x_send, x_recv, y_send, y_recv, z_send, z_recv, fin, fin_recv,
+    normed_all, grads_t, grads_late, mixed, acc, half_send, half_recv,
+    x_send, x_recv, kept, y_send, y_recv, z_send, z_recv, fin, fin_recv,
     code_ss, code_rs, halo_ss, halo_rs, head_ss, head_rs, back_ss, back_rs, top_ss, top_rs,
+    load_x, load_g, load_w, load_h,
     half_ss, half_rs, x_ss, x_rs, y_ss, y_rs, z_ss, z_rs, fin_ss, fin_rs,
 ):
-    tables, _, cols, wide = x.shape
-    width = g.shape[-1]
+    tables, _, cols, wide = x_in.shape
+    width = g_in.shape[-1]
     per_table = cols // CHUNK
     chunks = tables * per_table
     per_band = cols // BANDS // STEP
@@ -52,6 +54,18 @@
             src_ref=src, dst_ref=dst, send_sem=ss, recv_sem=rs, device_id=where, device_id_type=MESH
         )
 
+    def loads(t):
+        return (
+            pltpu.make_async_copy(x_in.at[t], x.at[t], load_x.at[t]),
+            pltpu.make_async_copy(g_in.at[t], g.at[t], load_g.at[t]),
+        )
+
+    weight_load = pltpu.make_async_copy(w_in, w, load_w)
+    weight_load.start()
+    for t in range(tables):
+        for one in loads(t):
+            one.start()
+
     barrier = pltpu.get_barrier_semaphore()
     for k in range(1, BANDS):
         pl.semaphore_signal(
@@ -77,23 +91,23 @@
     def head_copy(c, to):
         t, at = place(c)
         return copy(
-            x.at[t, pl.ds(0, 1), at], hx.at[t, :, at], head_ss.at[to - 1, c], head_rs.at[c], band=to
+            x_in.at[t, pl.ds(0, 1), at], hx.at[t, :, at], head_ss.at[to - 1, c], head_rs.at[c], band=to
         )
 
     def up_copies(c, to):
         t, at = place(c)
         rows = pl.ds(BAND - LOW, LOW)
         return (
-            copy(x.at[t, rows, at], lx.at[t, :, at], halo_ss.at[0, c], halo_rs.at[0, c], band=to),
-            copy(g.at[t, rows, at], lg.at[t, :, at], halo_ss.at[1, c], halo_rs.at[1, c], band=to),
+            copy(x_in.at[t, rows, at], lx.at[t, :, at], halo_ss.at[0, c], halo_rs.at[0, c], band=to),
+            copy(g_in.at[t, rows, at], lg.at[t, :, at], halo_ss.at[1, c], halo_rs.at[1, c], band=to),
         )
 
     def down_copies(c, to):
         t, at = place(c)
         rows = pl.ds(0, HIGH)
         return (
-            copy(x.at[t, rows, at], ux.at[t, :, at], halo_ss.at[2, c], halo_rs.at[2, c], band=to),
-            copy(g.at[t, rows, at], ug.at[t, :, at], halo_ss.at[3, c], halo_rs.at[3, c], band=to),
+            copy(x_in.at[t, rows, at], ux.at[t, :, at], halo_ss.at[2, c], halo_rs.at[2, c], band=to),
+            copy(g_in.at[t, rows, at], ug.at[t, :, at], halo_ss.at[3, c], halo_rs.at[3, c], band=to),
         )
 
     def back_low(c, to):
@@ -140,7 +154,11 @@
 
     @pl.when(band == 0)
     def _():
-        hx[...] = x[:, 0:1]
+        for t in range(tables):
+            own = pltpu.make_async_copy(x_in.at[t, pl.ds(0, 1)], hx.at[t], load_h)
+            own.start()
+            own.wait()
+
         lx[...] = jnp.zeros_like(lx)
         lg[...] = jnp.zeros_like(lg)
 
@@ -152,6 +170,7 @@
     for k in range(1, BANDS):
         code_arrival(k).wait_recv()
 
+    weight_load.wait()
     lane = lax.broadcasted_iota(jnp.int32, (1, 128), 1)
     left = jnp.where(lane < HD, 1.0, 0.0).astype(BF16)
     right = jnp.where(lane < HD, 0.0, 1.0).astype(BF16)
@@ -165,12 +184,19 @@
             [whole[:, s : s + SUB].reshape(CELLS, whole.shape[-1]) for s in range(0, STEP, SUB)], axis=0
         )
 
-    def step(t, at_step, many):
-        at = pl.ds(pl.multiple_of(at_step * STEP, STEP), STEP)
-        rows_all = pl.ds(pl.multiple_of(many * SLOTS * STEP, SLOTS * STEP), SLOTS * STEP)
+    def norms(t, at):
         states = flat((hx[t, :, at], lx[t, :, at], x[t, :, at], ux[t, :, at]))
         inverse = lax.rsqrt(jnp.mean(states * states, axis=-1, keepdims=True) + EPSILON)
-        scaled = states * inverse
+        return states * inverse, inverse
+
+    def cells(c):
+        return pl.ds(pl.multiple_of(c * SLOTS * STEP, SLOTS * STEP), SLOTS * STEP)
+
+    def grads_of(c):
+        t, at = place(c)
+        at_step = lax.rem(c, per_table)
+        scaled, inverse = norms(t, at)
+        rows_all = cells(c)
         normed = scaled.astype(BF16)
         normed_all[rows_all] = normed
         mixed[...] = dot(normed, w[...], 1, 0).astype(BF16)
@@ -230,7 +256,12 @@
             ],
             axis=0,
         )
-        grads_all[rows_all] = joined
+        turned = joined.T
+        grads_t[:, rows_all] = turned
+        return scaled, inverse, joined
+
+    def finish(c, scaled, inverse, joined):
+        t, at = place(c)
         normed_grad = dot(joined, w[...], 1, 1)
         coupling = jnp.mean(normed_grad * scaled, axis=-1, keepdims=True)
         result = inverse * (normed_grad - scaled * coupling)
@@ -241,33 +272,6 @@
         out[t, :, at] = result[1 + LOW : 1 + LOW + BAND]
         ux[t, :, at] = result[1 + LOW + BAND :]
 
-    steps = CHUNK // STEP
-
-    def work_chunk(c, carry):
-        @pl.when(band > 0)
-        def _():
-            head_copy(c, 1).wait_recv()
-
-        @pl.when(has_low)
-        def _():
-            for one in up_copies(c, 0):
-                one.wait_recv()
-
-        @pl.when(has_high)
-        def _():
-            for one in down_copies(c, 0):
-                one.wait_recv()
-
-        @pl.when(c + AHEAD < chunks)
-        def _():
-            send_chunk(c + AHEAD, 0)
-
-        def one_step(i, carry):
-            step(c // per_table, lax.rem(c, per_table) * steps + i, c * steps + i)
-            return carry
-
-        lax.fori_loop(0, steps, one_step, 0)
-
         @pl.when(has_low)
         def _():
             back_low(c, band - 1).start()
@@ -282,11 +286,55 @@
             def _():
                 back_head(c, source).start()
 
+    def arrive(c):
+        @pl.when(lax.rem(c, per_table) == 0)
+        def _():
+            for one in loads(c // per_table):
+                one.wait()
+
+        @pl.when(band > 0)
+        def _():
+            head_copy(c, 1).wait_recv()
+
+        @pl.when(has_low)
+        def _():
+            for one in up_copies(c, 0):
+                one.wait_recv()
+
+        @pl.when(has_high)
+        def _():
+            for one in down_copies(c, 0):
+                one.wait_recv()
+
+        @pl.when(c + AHEAD < chunks)
+        def _():
+            send_chunk(c + AHEAD, 0)
+
+    early = chunks - LATE
+
+    def work_early(c, carry):
+        arrive(c)
+        finish(c, *grads_of(c))
         return carry
 
-    lax.fori_loop(0, chunks, work_chunk, 0)
-
-    total_rows = grads_all.shape[0]
+    def work_late(c, carry):
+        arrive(c)
+        grads_late[cells(c - early)] = grads_of(c)[2]
+        return carry
+
+    def end_late(c, carry):
+        t, at = place(c)
+        scaled, inverse = norms(t, at)
+        finish(c, scaled, inverse, grads_late[cells(c - early)])
+        return carry
+
+    def late(n):
+        lax.fori_loop(early + n, early + n + 1, end_late, 0)
+
+    lax.fori_loop(0, early, work_early, 0)
+    lax.fori_loop(early, chunks, work_late, 0)
+
+    total_rows = normed_all.shape[0]
     block = 3 * width // SHARES
     rows_half = SHARES // 2 * block
     mine = pl.ds(pl.multiple_of(core * rows_half, 16), rows_half)
@@ -297,7 +345,7 @@
 
         def deep(i, carry):
             at = pl.ds(pl.multiple_of(i * DEEP, DEEP), DEEP)
-            acc[n] += dot(grads_all[at, :], normed_all[at, lanes], 0, 0)
+            acc[n] += dot(grads_t[:, at], normed_all[at, lanes], 1, 0)
             return carry
 
         lax.fori_loop(begin, end, deep, 0)
@@ -326,6 +374,58 @@
     half_send[1] = acc[1, theirs, :].astype(BF16)
     half_copy(1).start()
 
+    def y_copy(j):
+        return copy(y_send.at[j], y_recv.at[j], y_ss.at[j], y_rs.at[j], dp=z * 2 + 1 - y)
+
+    late(0)
+    half_copy(1).wait_recv()
+    for j in range(2):
+        x_copy(j).wait_recv()
+        whole = acc[1, piece(j), :] + half_recv[1, 2 * block * j : 2 * block * (j + 1)].astype(F32)
+        whole = (whole + x_recv[j].astype(F32)).reshape(2, block, wide // 2)
+        kept[j] = jnp.where(y == 0, whole[0], whole[1])
+        y_send[j] = jnp.where(y == 0, whole[1], whole[0]).astype(BF16)
+        y_copy(j).start()
+
+    def z_copy(j, source):
+        return copy(z_send.at[j], z_recv.at[source], z_ss.at[j], z_rs.at[source], dp=(2 * core + j) * 2 + y)
+
+    zs = SHARES // 2
+    late(1)
+    for j in range(2):
+        y_copy(j).wait_recv()
+        kept[j] += y_recv[j].astype(F32)
+        z_send[j] = kept[j].astype(BF16)
+        for source in range(zs):
+
+            @pl.when((z == source) & (2 * core + j != z))
+            def _():
+                z_copy(j, source).start()
+
+    fin_copy = copy(fin, fin_recv, fin_ss, fin_rs, band=sibling)
+    holder = z // 2 == core
+
+    def emit(full):
+        half = wide // 4
+        wout[...] = jnp.where(core == 0, full[:, :half], full[:, half:])
+
+    late(2)
+
+    @pl.when(holder)
+    def _():
+        fin[...] = jnp.where(lax.rem(z, 2) == 0, kept[0], kept[1])
+        for source in range(zs):
+
+            @pl.when(z != source)
+            def _():
+                z_copy(0, source).wait_recv()
+                fin[...] += z_recv[source].astype(F32)
+
+        fin_copy.start()
+        emit(fin[...])
+
+    late(3)
+
     def merge_chunk(c, carry):
         t, at = place(c)
 
@@ -353,53 +453,8 @@
 
     lax.fori_loop(0, chunks, merge_chunk, 0)
 
-    def y_copy(j):
-        return copy(y_send.at[j], y_recv.at[j], y_ss.at[j], y_rs.at[j], dp=z * 2 + 1 - y)
-
-    half_copy(1).wait_recv()
-    kept_y = []
-    for j in range(2):
-        x_copy(j).wait_recv()
-        kept = acc[1, piece(j), :] + half_recv[1, 2 * block * j : 2 * block * (j + 1)].astype(F32)
-        kept = (kept + x_recv[j].astype(F32)).reshape(2, block, wide // 2)
-        kept_y.append(jnp.where(y == 0, kept[0], kept[1]))
-        y_send[j] = jnp.where(y == 0, kept[1], kept[0]).astype(BF16)
-        y_copy(j).start()
-
-    def z_copy(j, source):
-        return copy(z_send.at[j], z_recv.at[source], z_ss.at[j], z_rs.at[source], dp=(2 * core + j) * 2 + y)
-
-    zs = SHARES // 2
-    acc_z = []
-    for j in range(2):
-        y_copy(j).wait_recv()
-        acc_z.append(kept_y[j] + y_recv[j].astype(F32))
-        z_send[j] = acc_z[j].astype(BF16)
-        for source in range(zs):
-
-            @pl.when((z == source) & (2 * core + j != z))
-            def _():
-                z_copy(j, source).start()
-
-    fin_copy = copy(fin, fin_recv, fin_ss, fin_rs, band=sibling)
-    holder = z // 2 == core
-
-    def emit(full):
-        half = wide // 4
-        wout[...] = jnp.where(core == 0, full[:, :half], full[:, half:])
-
     @pl.when(holder)
     def _():
-        fin[...] = jnp.where(lax.rem(z, 2) == 0, acc_z[0], acc_z[1])
-        for source in range(zs):
-
-            @pl.when(z != source)
-            def _():
-                z_copy(0, source).wait_recv()
-                fin[...] += z_recv[source].astype(F32)
-
-        fin_copy.start()
-        emit(fin[...])
         fin_copy.wait_send()
 
     @pl.when(jnp.logical_not(holder))
@@ -493,25 +548,30 @@
     vmem = pl.BlockSpec(memory_space=pltpu.VMEM)
     input_grad, turned = pl.pallas_call(
         kernel,
-        in_specs=[vmem] * 4,
+        in_specs=[vmem] + [pl.BlockSpec(memory_space=pl.ANY)] * 3,
         out_specs=[vmem] * 2,
         out_shape=[
             jax.ShapeDtypeStruct(cell_states.shape, BF16),
             jax.ShapeDtypeStruct((block, wide // BANDS), F32),
         ],
         scratch_shapes=[
+            pltpu.VMEM(cell_states.shape, BF16),
+            pltpu.VMEM(head_grads.shape, BF16),
+            pltpu.VMEM(proj_weights.shape, BF16),
             pltpu.VMEM(codes.shape, jnp.int32),
             halo(1, wide), halo(LOW, wide), halo(HIGH, wide), halo(LOW, width), halo(HIGH, width),
             halo(LOW, wide), halo(HIGH, wide),
             pltpu.VMEM((BANDS - 1, tables, 1, cols, wide), BF16),
             pltpu.VMEM((many, wide), BF16),
-            pltpu.VMEM((many, 3 * width), BF16),
+            pltpu.VMEM((3 * width, many), BF16),
+            pltpu.VMEM((LATE * SLOTS * STEP, 3 * width), BF16),
             pltpu.VMEM((SLOTS * STEP, 3 * width), BF16),
             pltpu.VMEM((2, 3 * width, lanes), F32),
             pltpu.VMEM((2, rows_half, lanes), BF16),
             pltpu.VMEM((2, rows_half, lanes), BF16),
             pltpu.VMEM((2, 2 * block, lanes), BF16),
             pltpu.VMEM((2, 2 * block, lanes), BF16),
+            pltpu.VMEM((2, block, lanes), F32),
             pltpu.VMEM((2, block, lanes), BF16),
             pltpu.VMEM((2, block, lanes), BF16),
             pltpu.VMEM((2, block, lanes), BF16),
@@ -523,6 +583,7 @@
             sems(BANDS - 1, chunks), sems(chunks),
             *pair(2, chunks),
             sems(chunks), sems(BANDS - 1, chunks),
+            sems(tables), sems(tables), one, one,
             *pair(2),
             *pair(2),
             *pair(2),

time: 97.6 us -> 96.2 us (0.986)
  the two profiles are of different devices: /device:TPU:9 before, /device:TPU:0 now
where the time goes in v4:
time: 96.2 us; the launch traced here: 95.9 us
  Pallas kernels  85.9 us (89%)
  local copies, waits for them, and re-layouts  8.31 us (9%)
    pallas_call x1, Pallas kernels, halo_body(): pl.pallas_call(kernel, in_specs=[vmem] + [pl.BlockSpec(memory_space=pl.AN...  85.9 us
    unnamed x13, local copies, waits for them, and re-layouts  6.1 us

profile of v4, /device:TPU:0, one launch (start us, length us, event | category | flops | bytes accessed | tf_op | source)
XLA Modules:
  0.0 95.9 jit_solution(10955446316514434737)
XLA Ops:
  0.7 0.1 add.124
  0.8 0.8 copy.29
  1.7 0.1 multiply_add_fusion
  1.8 0.1 copy.46
  1.9 0.1 pad_bitcast_fusion.7
  2.0 0.1 and_select_fusion.3
  2.1 0.1 copy.47
  2.2 0.1 pad_bitcast_fusion.6
  2.2 0.1 copy.33
  2.3 0.1 reshape.96
  2.4 0.1 copy.51
  2.5 0.1 pad_bitcast_fusion.2
  2.6 0.1 copy.41
  2.7 0.1 reshape.104
  2.8 0.1 copy.49
  2.9 0.1 pad_bitcast_fusion.4
  2.9 0.1 copy.37
  3.0 0.1 reshape.100
  3.1 0.1 copy.53
  3.2 0.1 pad_bitcast_fusion
  3.3 0.1 copy.45
  3.4 0.1 reshape.108
  3.5 0.1 copy.31
  3.6 0.1 reshape.94
  3.7 0.1 copy.48
  3.8 0.1 pad_bitcast_fusion.5
  3.9 0.1 copy.35
  3.9 0.1 reshape.98
  4.1 0.1 copy.50
  4.2 0.1 pad_bitcast_fusion.3
  4.2 0.1 copy.39
  4.3 0.1 reshape.102
  4.4 0.1 copy.52
  4.5 0.1 pad_bitcast_fusion.1
  4.6 0.1 copy.43
  4.7 0.1 reshape.106
  4.8 0.6 pad_add_fusion.code_in
  5.4 85.9 %shard_map.59 = (bf16[2,8,128,768]{3,2,1,0:T(8,128)(2,1)}, f32[144,192]{1,0:T(8,128)}) custom-call(s32[4,2,1,8,128]{4,3,2,1,0:T(8,128)} %pad_add_fusion.code_in, bf16[2,8,128,768]{3,2,1,0:T(8,128)(2,1)} %x_in.1, bf16[2,8,128,384]{3,2,1,0:T(8,128)(2,1)} %g_in.1, bf16[768,1152]{1,0:T(8,128)(2,1)} %w_in.1), custom_call_target="tpu_custom_call" | custom-call | flops 25769803776 | bytes 7864320 | tf_op jit(solution)/shard_map/pallas_call | solution.py:549
  91.3 0.0 copy-start
  91.3 3.9 %copy.56 = bf16[2,8,128,768]{3,2,1,0:T(8,128)(2,1)} copy(bf16[2,8,128,768]{3,2,1,0:T(8,128)(2,1)} %get-tuple-element.34) | data formatting | bytes 6291456
  95.2 0.0 copy-done
  95.2 0.7 copy.57
  (15 shorter events, 0.2 us)
Async XLA Ops:
  91.3 3.9 %copy-start = (f32[144,192]{1,0:T(8,128)S(1)}, f32[144,192]{1,0:T(8,128)}, u32[]{:S(2)}) copy-start(f32[144,192]{1,0:T(8,128)} %get-tuple-element.5) | copy-start | bytes 331780

commit v5 on v4

--- a/solution.py
+++ b/solution.py
@@ -31,7 +31,7 @@
 
 
 def kernel(
-    code_in, x_in, g_in, w_in, out, wout, x, g, w,
+    code_in, x_in, g_in, w_in, out, wout, x, g, w, w_turned,
     code, hx, lx, ux, lg, ug, from_high, from_low, from_head,
     normed_all, grads_t, grads_late, mixed, acc, half_send, half_recv,
     x_send, x_recv, kept, y_send, y_recv, z_send, z_recv, fin, fin_recv,
@@ -167,10 +167,12 @@
         ux[...] = jnp.zeros_like(ux)
         ug[...] = jnp.zeros_like(ug)
 
+    weight_load.wait()
+    w_turned[...] = w[...].T
+
     for k in range(1, BANDS):
         code_arrival(k).wait_recv()
 
-    weight_load.wait()
     lane = lax.broadcasted_iota(jnp.int32, (1, 128), 1)
     left = jnp.where(lane < HD, 1.0, 0.0).astype(BF16)
     right = jnp.where(lane < HD, 0.0, 1.0).astype(BF16)
@@ -262,7 +264,7 @@
 
     def finish(c, scaled, inverse, joined):
         t, at = place(c)
-        normed_grad = dot(joined, w[...], 1, 1)
+        normed_grad = dot(joined, w_turned[...], 1, 0)
         coupling = jnp.mean(normed_grad * scaled, axis=-1, keepdims=True)
         result = inverse * (normed_grad - scaled * coupling)
         pieces = [result[s * CELLS : (s + 1) * CELLS].reshape(SLOTS, SUB, wide) for s in range(STEP // SUB)]
@@ -558,6 +560,7 @@
             pltpu.VMEM(cell_states.shape, BF16),
             pltpu.VMEM(head_grads.shape, BF16),
             pltpu.VMEM(proj_weights.shape, BF16),
+            pltpu.VMEM((3 * width, wide), BF16),
             pltpu.VMEM(codes.shape, jnp.int32),
             halo(1, wide), halo(LOW, wide), halo(HIGH, wide), halo(LOW, width), halo(HIGH, width),
             halo(LOW, wide), halo(HIGH, wide),

time: 96.2 us -> 96.1 us (level)
  no operation moved by 1% of the time
where the time goes in v5:
time: 96.1 us; the launch traced here: 95.8 us
  Pallas kernels  85.8 us (89%)
  local copies, waits for them, and re-layouts  8.31 us (9%)
    pallas_call x1, Pallas kernels, halo_body(): pl.pallas_call(kernel, in_specs=[vmem] + [pl.BlockSpec(memory_space=pl.AN...  85.8 us
    unnamed x13, local copies, waits for them, and re-layouts  6.1 us

profile of v5, /device:TPU:0, one launch (start us, length us, event | category | flops | bytes accessed | tf_op | source)
XLA Modules:
  0.0 95.8 jit_solution(17956979577962608781)
XLA Ops:
  0.7 0.1 add.124
  0.8 0.8 copy.29
  1.7 0.1 multiply_add_fusion
  1.8 0.1 copy.46
  1.9 0.1 pad_bitcast_fusion.7
  2.0 0.1 and_select_fusion.3
  2.1 0.1 copy.47
  2.2 0.1 pad_bitcast_fusion.6
  2.2 0.1 copy.33
  2.3 0.1 reshape.96
  2.4 0.1 copy.51
  2.5 0.1 pad_bitcast_fusion.2
  2.6 0.1 copy.41
  2.7 0.1 reshape.104
  2.8 0.1 copy.49
  2.9 0.1 pad_bitcast_fusion.4
  2.9 0.1 copy.37
  3.0 0.1 reshape.100
  3.1 0.1 copy.53
  3.2 0.1 pad_bitcast_fusion
  3.3 0.1 copy.45
  3.4 0.1 reshape.108
  3.5 0.1 copy.31
  3.6 0.1 reshape.94
  3.7 0.1 copy.48
  3.8 0.1 pad_bitcast_fusion.5
  3.9 0.1 copy.35
  3.9 0.1 reshape.98
  4.1 0.1 copy.50
  4.2 0.1 pad_bitcast_fusion.3
  4.2 0.1 copy.39
  4.3 0.1 reshape.102
  4.4 0.1 copy.52
  4.5 0.1 pad_bitcast_fusion.1
  4.6 0.1 copy.43
  4.7 0.1 reshape.106
  4.8 0.6 pad_add_fusion.code_in
  5.4 85.8 %shard_map.59 = (bf16[2,8,128,768]{3,2,1,0:T(8,128)(2,1)}, f32[144,192]{1,0:T(8,128)}) custom-call(s32[4,2,1,8,128]{4,3,2,1,0:T(8,128)} %pad_add_fusion.code_in, bf16[2,8,128,768]{3,2,1,0:T(8,128)(2,1)} %x_in.1, bf16[2,8,128,384]{3,2,1,0:T(8,128)(2,1)} %g_in.1, bf16[768,1152]{1,0:T(8,128)(2,1)} %w_in.1), custom_call_target="tpu_custom_call" | custom-call | flops 25769803776 | bytes 7864320 | tf_op jit(solution)/shard_map/pallas_call | solution.py:551
  91.3 0.0 copy-start
  91.3 3.9 %copy.56 = bf16[2,8,128,768]{3,2,1,0:T(8,128)(2,1)} copy(bf16[2,8,128,768]{3,2,1,0:T(8,128)(2,1)} %get-tuple-element.34) | data formatting | bytes 6291456
  95.1 0.0 copy-done
  95.1 0.7 copy.57
  (15 shorter events, 0.2 us)
Async XLA Ops:
  91.3 3.9 %copy-start = (f32[144,192]{1,0:T(8,128)S(1)}, f32[144,192]{1,0:T(8,128)}, u32[]{:S(2)}) copy-start(f32[144,192]{1,0:T(8,128)} %get-tuple-element.5) | copy-start | bytes 331780
